TPU v7x, 128 devices: a whole 4x4x4 slice. The times are simulated.
128 devices in a mesh: group: 16 (over z, x_lo, core), tp: 8 (over y, x_hi).
Axes of the slice: x: 4 (x_hi: 2, x_lo: 2; x = x_hi * 2 + x_lo), y: 4, z: 4, core: 2. Of those that a mesh axis runs over, the one named last changes fastest.
Arguments:
- dec_rows: bfloat16 [224, 5120], P('group'), may hold values from -6 to 6
- kv_cache: bfloat16 [224, 2, 768, 1024], P('group', None, None, 'tp'), may hold values from -40 to 40
- lengths: int32 [224], replicated, may hold values from 1 to 766, as said below
- dest_group: int32 [224], replicated, may hold values from 0 to 15, as said below
- dest_slot: int32 [224], replicated, may hold values from 0 to 13, as said below
- score_rows: bfloat16 [7168, 5120], P(('group', 'tp')), may hold values from -6 to 6
- doc_ids: int32 [16, 448], P('group'), may hold values from 0 to 8, never falling along the last dimension, each value on 1 to 336 neighbouring positions
- norm_gain: float32 [5120], replicated, may hold values from 0.1 to 1.9
- query_gain: float32 [128], replicated, may hold values from 0.5 to 42
- key_gain: float32 [128], replicated, may hold values from 0.5 to 42
- w_query: bfloat16 [5120, 4096], P(None, 'tp'), may hold values from -0.078125 to 0.078125
- w_keyval: bfloat16 [5120, 2, 1024], P(None, None, 'tp'), may hold values from -0.078125 to 0.078125
- w_out: bfloat16 [4096, 5120], P('tp'), may hold values from -0.09375 to 0.09375
Outputs:
- dec_out: bfloat16 [224, 5120], P('group')
- dec_cache: bfloat16 [224, 2, 768, 1024], P('group', None, None, 'tp')
- score_out: bfloat16 [7168, 5120], P(('group', 'tp'))
Inputs may be any that keep to these rules, and one draw needn't show every extreme that they name: `lengths`: every decode row has room for two more positions; some row has exactly 766 cached positions. `dest_group`: A group sends either none or exactly 1 of its rows to any one group (possibly itself), and every group receives exactly 14 rows in all. `dest_slot`: the rows that reach one group take its slots 0 to 13, each slot once.
All inputs are finite; a program needn't handle non-finite values.
Results may differ from a plain program's by a relative error of at most 0.03615.
The roundings to bfloat16 on the way count: a program that leaves them out, or rounds other values in their place, can miss the bound.
Values may be sent and summed in bfloat16 or wider, within the bound.
A program may use at most 128 MiB of HBM per device.

v0:
```python
import math

import jax
import jax.numpy as jnp
from jax import lax
from jax.sharding import PartitionSpec as P

HD = 128


EPS = 1e-06


def row_scale(wide):
    return lax.rsqrt(jnp.mean(wide * wide, axis=-1, keepdims=True) + EPS)


def project_rows(rows, norm_gain, w_query, w_keyval):
    wide = rows.astype(jnp.float32)
    scale = row_scale(wide)
    normed = (wide * norm_gain).astype(jnp.bfloat16)
    query = jnp.dot(normed, w_query, preferred_element_type=jnp.float32) * scale
    flat = w_keyval.reshape(w_keyval.shape[0], -1)
    keyval = jnp.dot(normed, flat, preferred_element_type=jnp.float32) * scale
    return (query, keyval)


def head_norm(vectors, gain):
    return (vectors * row_scale(vectors) * gain).astype(jnp.bfloat16)


def softmax_rows(scores):
    top = jnp.max(scores, axis=-1, keepdims=True)
    expo = jnp.exp(scores - top)
    return (expo / jnp.sum(expo, axis=-1, keepdims=True)).astype(jnp.bfloat16)


def residual_update(rows, partial_value):
    summed = lax.psum(partial_value, "tp")
    return (rows.astype(jnp.float32) + summed).astype(jnp.bfloat16)


def decode_steps(rows, cache, lengths, norm_gain, query_gain, key_gain, w_query, w_keyval, w_out):
    count = rows.shape[0]
    ctx = cache.shape[2]
    width = cache.shape[3]
    kv_local = width // HD
    for step in range(2):
        positions = lengths + step
        query, keyval = project_rows(rows, norm_gain, w_query, w_keyval)
        group = query.shape[1] // width
        heads = head_norm(query.reshape(count, kv_local, group, HD), query_gain)
        new_keys = head_norm(keyval[:, :width].reshape(count, kv_local, HD), key_gain)
        new_vals = keyval[:, width:].astype(jnp.bfloat16).reshape(count, 1, width)
        spots = lax.broadcasted_iota(jnp.int32, (count, ctx, 1), 1) == positions[:, None, None]
        keys = jnp.where(spots, new_keys, cache[:, 0])
        vals = jnp.where(spots, new_vals, cache[:, 1])
        cache = jnp.stack([keys, vals], axis=1)
        scores = jnp.einsum(
            "nkgd,nckd->nkgc",
            heads,
            keys.reshape(count, ctx, kv_local, HD),
            preferred_element_type=jnp.float32,
        ) * (1.0 / math.sqrt(HD))
        live = (
            lax.broadcasted_iota(jnp.int32, (count, 1, 1, ctx), 3) <= positions[:, None, None, None]
        )
        weights = softmax_rows(jnp.where(live, scores, -jnp.inf))
        attn = jnp.einsum(
            "nkgc,nckd->nkgd",
            weights,
            vals.reshape(count, ctx, kv_local, HD),
            preferred_element_type=jnp.float32,
        )
        attn = attn.astype(jnp.bfloat16).reshape(count, -1)
        partial_value = jnp.dot(attn, w_out, preferred_element_type=jnp.float32)
        rows = residual_update(rows, partial_value)
    return (rows, cache)


def send_plan(dest_local, ngroup, most):
    count = dest_local.shape[0]
    earlier = lax.broadcasted_iota(jnp.int32, (count, count), 1) < lax.broadcasted_iota(
        jnp.int32, (count, count), 0
    )
    same = dest_local[None, :] == dest_local[:, None]
    rank = jnp.sum((same & earlier).astype(jnp.int32), axis=1)
    target = dest_local * most + rank
    slots = lax.broadcasted_iota(jnp.int32, (ngroup * most, count), 0)
    match = slots == target[None, :]
    filled = jnp.any(match, axis=1)
    picks = jnp.sum(
        jnp.where(match, lax.broadcasted_iota(jnp.int32, (ngroup * most, count), 1), 0), axis=1
    )
    return (picks, filled)


def receive_plan(dest_all, slot_all, len_all, me, ngroup, count, most):
    grid = dest_all.reshape(ngroup, count)
    earlier = lax.broadcasted_iota(jnp.int32, (count, count), 1) < lax.broadcasted_iota(
        jnp.int32, (count, count), 0
    )
    same = grid[:, None, :] == grid[:, :, None]
    rank = jnp.sum((same & earlier[None]).astype(jnp.int32), axis=2)
    arrival = (lax.broadcasted_iota(jnp.int32, (ngroup, count), 0) * most + rank).reshape(-1)
    match = (dest_all[None, :] == me) & (
        slot_all[None, :] == lax.broadcasted_iota(jnp.int32, (count, 1), 0)
    )
    where_from = jnp.sum(jnp.where(match, arrival[None, :], 0), axis=1)
    length = jnp.sum(jnp.where(match, len_all[None, :], 0), axis=1)
    return (where_from, length)


def pack_for_send(rows, cache, dest_local, ngroup, most):
    picks, filled = send_plan(dest_local, ngroup, most)
    send_cache = jnp.where(
        filled[:, None, None, None], jnp.take(cache, picks, axis=0), jnp.zeros((), cache.dtype)
    )
    send_rows = jnp.where(filled[:, None], jnp.take(rows, picks, axis=0), jnp.zeros((), rows.dtype))
    send_cache = send_cache.reshape((ngroup, most) + cache.shape[1:])
    send_rows = send_rows.reshape(ngroup, most, rows.shape[1])
    return (send_cache, send_rows)


def per_device(
    dec_rows,
    kv_cache,
    lengths,
    dest_group,
    dest_slot,
    score_rows,
    doc_ids,
    norm_gain,
    query_gain,
    key_gain,
    w_query,
    w_keyval,
    w_out,
):
    ngroup = lax.axis_size("group")
    me = lax.axis_index("group")
    count = dec_rows.shape[0]
    most = (count + ngroup - 1) // ngroup
    dest_local = lax.dynamic_slice_in_dim(dest_group, me * count, count)
    where_from, slot_lengths = receive_plan(dest_group, dest_slot, lengths, me, ngroup, count, most)
    send_cache, send_rows = pack_for_send(dec_rows, kv_cache, dest_local, ngroup, most)
    got_cache, got_rows = (
        lax.all_to_all(send_cache, "group", split_axis=0, concat_axis=0, tiled=True),
        lax.all_to_all(send_rows, "group", split_axis=0, concat_axis=0, tiled=True),
    )
    cache_here = jnp.take(
        got_cache.reshape((ngroup * most,) + kv_cache.shape[1:]), where_from, axis=0
    )
    rows_here = jnp.take(got_rows.reshape(ngroup * most, dec_rows.shape[1]), where_from, axis=0)
    dec_out, dec_cache = decode_steps(
        rows_here,
        cache_here,
        slot_lengths,
        norm_gain,
        query_gain,
        key_gain,
        w_query,
        w_keyval,
        w_out,
    )
    width = w_keyval.shape[2]
    kv_local = width // HD
    query, keyval = project_rows(
        lax.all_gather(score_rows, "tp", axis=0, tiled=True), norm_gain, w_query, w_keyval
    )
    projected = jnp.concatenate([query, keyval], axis=1)
    tokens = projected.shape[0]
    query_cols = w_query.shape[1]
    group = query_cols // width
    heads = head_norm(projected[:, :query_cols].reshape(tokens, kv_local, group, HD), query_gain)
    keys = head_norm(
        projected[:, query_cols : query_cols + width].reshape(tokens, kv_local, HD), key_gain
    )
    vals = projected[:, query_cols + width :].astype(jnp.bfloat16).reshape(tokens, kv_local, HD)
    docs = doc_ids[0]
    scores = jnp.einsum("pkgd,qkd->kgpq", heads, keys, preferred_element_type=jnp.float32) * (
        1.0 / math.sqrt(HD)
    )
    later = lax.broadcasted_iota(jnp.int32, (tokens, tokens), 1) <= lax.broadcasted_iota(
        jnp.int32, (tokens, tokens), 0
    )
    live = (docs[:, None] == docs[None, :]) & later
    weights = softmax_rows(jnp.where(live[None, None], scores, -jnp.inf))
    attn = jnp.einsum("kgpq,qkd->pkgd", weights, vals, preferred_element_type=jnp.float32)
    attn = attn.astype(jnp.bfloat16).reshape(tokens, -1)
    summed = lax.psum_scatter(
        jnp.dot(attn, w_out, preferred_element_type=jnp.float32).astype(jnp.bfloat16),
        "tp",
        scatter_dimension=0,
        tiled=True,
    ).astype(jnp.float32)
    score_out = (score_rows.astype(jnp.float32) + summed).astype(jnp.bfloat16)
    return (dec_out, dec_cache, score_out)


def solution(mesh):
    placed = (
        P("group", None),
        P("group", None, None, "tp"),
        P(),
        P(),
        P(),
        P(("group", "tp"), None),
        P("group", None),
        P(),
        P(),
        P(),
        P(None, "tp"),
        P(None, None, "tp"),
        P("tp", None),
    )
    return jax.shard_map(
        per_device,
        mesh=mesh,
        in_specs=placed,
        out_specs=(P("group", None), P("group", None, None, "tp"), P(("group", "tp"), None)),
        check_vma=False,
    )
```

profile of v0, /device:TPU:0, one launch (start us, length us, event | category | flops | bytes accessed | tf_op | source)
XLA Modules:
  0.0 475.1 jit_solution(15514789798754639620)
XLA Ops:
  7.2 0.8 dynamic_slice.3
  8.2 0.8 dynamic-slice_add_fusion
  9.2 0.6 gather_fusion
  9.9 0.5 broadcast.505
  10.4 0.7 reduce.22
  11.2 0.8 reshape.612
  11.9 6.4 %all-to-all-start = ((bf16[16,2,2560]{2,1,0:T(2,128)(2,1)}), bf16[16,2,2560]{2,1,0:T(2,128)(2,1)S(1)}, u32[]{:S(2)}, u32[]{:S(2)}) async-start(bf16[16,2,2560]{2,1,0:T(2,128)(2,1)} %reshape.612), calls=%async_computation | async-start | bytes 327680 | tf_op jit(solution)/shard_map/all_to_all | solution.py:149
  18.4 6.6 %gather_fusion.2 = bf16[16,2,768,128]{3,2,1,0:T(8,128)(2,1)} fusion(bf16[14,2,768,128]{3,2,1,0:T(8,128)(2,1)} %param.14, s32[1024]{0:T(1024)S(1)} %pad_clamp_fusion.1), kind=kCustom, calls=%fused_computation.2 | custom fusion | bytes 12582976 | tf_op jit(solution)/shard_map/jit(_take)/gather | solution.py:117
  24.9 6.2 %fusion.4 = bf16[16,1,2,768,128]{4,3,2,1,0:T(8,128)(2,1)} fusion(bf16[16,2,768,128]{3,2,1,0:T(8,128)(2,1)} %gather_fusion.2, pred[16]{0:T(512)(128)(4,1)S(1)} %compare_and_fusion, pred[16]{0:T(512)(128)(4,1)S(1)} %fusion.105), kind=kLoop, calls=%fused_computation.12 | loop fusion | flops 6291456 | bytes 12582944 | tf_op jit(solution)/shard_map/jit(_where)/select_n | solution.py:116
  31.2 5.9 %all-to-all-start.1 = ((bf16[16,1,2,768,128]{4,3,2,1,0:T(8,128)(2,1)}), bf16[16,1,2,768,128]{4,3,2,1,0:T(8,128)(2,1)}, u32[]{:S(2)}, u32[]{:S(2)}) async-start(bf16[16,1,2,768,128]{4,3,2,1,0:T(8,128)(2,1)} %fusion.4), calls=%async_computation.1 | async-start | bytes 12582912 | tf_op jit(solution)/shard_map/all_to_all | solution.py:148
  37.3 0.4 convert_reduce_fusion
  38.4 0.6 gather_fusion.1
  39.0 0.2 fusion.82
  39.3 2.2 fusion.62
  41.6 3.3 fusion.111
  45.2 64.7 %all-to-all-done.1 = bf16[16,1,2,768,128]{4,3,2,1,0:T(8,128)(2,1)} async-done(((bf16[16,1,2,768,128]{4,3,2,1,0:T(8,128)(2,1)}), bf16[16,1,2,768,128]{4,3,2,1,0:T(8,128)(2,1)}, u32[]{:S(2)}, u32[]{:S(2)}) %all-to-all-start.1) | async-done | bytes 6291488 | tf_op jit(solution)/shard_map/all_to_all | solution.py:148
  109.9 6.6 %gather_fusion.3 = bf16[14,2,768,128]{3,2,1,0:T(8,128)(2,1)} fusion(bf16[16,2,768,128]{3,2,1,0:T(8,128)(2,1)} %bitcast.6, s32[1024]{0:T(1024)S(1)} %pad_clamp_fusion), kind=kCustom, calls=%fused_computation.3 | custom fusion | bytes 11010104 | tf_op jit(solution)/shard_map/jit(_take)/gather | solution.py:151
  116.5 5.6 %broadcast_select_fusion = bf16[14,2,768,128]{3,2,1,0:T(8,128)(2,1)} fusion(bf16[14,2,768,128]{3,2,1,0:T(8,128)(2,1)} %gather_fusion.3, pred[14]{0:T(512)(128)(4,1)S(1)} %compare_and_fusion.1), kind=kLoop, calls=%fused_computation.14 | loop fusion | flops 2752512 | bytes 11010062 | tf_op jit(solution)/shard_map/jit(_take)/select_n | solution.py:151
  122.1 3.5 fusion.112
  125.6 3.9 fusion.58
  129.6 4.0 fusion.118
  133.7 0.7 all-gather.2.cloned.1.call-update
  134.6 83.4 %all-reduce.3.cloned.1.call-done = f32[14,5120]{1,0:T(8,128)} async-done(((f32[14,5120]{1,0:T(8,128)}), f32[14,5120]{1,0:T(8,128)}) %all-reduce.3.cloned.1.call-update) | async-done | bytes 286736 | tf_op jit(solution)/shard_map/psum | solution.py:39
  218.1 1.2 fusion.85
  219.3 2.2 fusion.65
  221.5 3.3 fusion.113
  225.1 7.2 %fusion.114 = (f32[14,4]{1,0:T(8,128)S(1)}, f32[14,4,768]{2,1,0:T(4,128)S(1)}) fusion(pred[14,768]{1,0:T(8,128)(4,1)S(1)} %get-tuple-element.10, bf16[14,2,768,128]{3,2,1,0:T(8,128)(2,1)} %broadcast_select_fusion, pred[14,768]{1,0:T(8,128)(4,1)S(1)} %get-tuple-element.25, bf16[14,128]{1,0:T(8,128)(2,1)S(1)} %multiply_convert_fusion.5, ...), kind=kOutput, calls=%fused_computation.162 | convolution fusion | flops 13956863 | bytes 2993600 | tf_op jit(solution)/shard_map/sub | solution.py:34
  232.3 6.5 %fusion.59 = bf16[14,4,128]{2,1,0:T(4,128)(2,1)S(1)} fusion(pred[14,768]{1,0:T(8,128)(4,1)S(1)} %get-tuple-element.10, bf16[14,2,768,128]{3,2,1,0:T(8,128)(2,1)} %broadcast_select_fusion, pred[14,768]{1,0:T(8,128)(4,1)S(1)} %get-tuple-element.25, bf16[14,128]{1,0:T(8,128)(2,1)S(1)} %slice.90, bf16[14,128]{1,0:T(8,128)(2,1)S(1)} %slice.91, ...), kind=kOutput, calls=%fused_computation.65 | convolution fusion | flops 13855744 | bytes 2967776 | tf_op jit(solution)/shard_map/nkgc,nckd->nkgd/dot_general | solution.py:69
  238.9 1.6 fusion.119
  240.8 52.2 %all-gather.2.cloned.1.call-done = bf16[448,5120]{1,0:T(8,128)(2,1)} async-done(((bf16[56,5120]{1,0:T(8,128)(2,1)}), bf16[448,5120]{1,0:T(8,128)(2,1)}) %all-gather.2.cloned.1.call-update) | async-done | bytes 4587536 | tf_op jit(solution)/shard_map/all_gather | solution.py:169
  293.0 3.4 fusion.3
  296.4 4.9 %fusion.45 = f32[448,256]{1,0:T(8,128)S(1)} fusion(bf16[640,8,2,128]{3,2,1,0:T(2,128)(2,1)} %bitcast.159, bf16[448,5120]{1,0:T(8,128)(2,1)} %all-gather.2.cloned.1.call-done, f32[5120]{0:T(1024)S(1)} %copy-done.5, f32[448]{0:T(512)S(1)} %add_rsqrt_fusion.4), kind=kOutput, calls=%fused_computation.54 | convolution fusion | flops 1181401088 | bytes 7689984 | tf_op jit(solution)/shard_map/dot_general | solution.py:24
  301.5 0.6 copy-done.3
  302.1 2.5 fusion.115
  304.7 0.3 mul.329
  305.0 0.5 reduce_sum.174
  305.6 0.5 mul.330
  306.2 1.9 fusion.10
  308.1 0.8 fusion.9
  308.9 1.4 fusion.42
  310.3 0.4 copy.58
  310.8 4.6 convolution_convert_fusion
  315.4 5.2 %select_select_fusion.1 = (bf16[14,1,768,128]{3,2,1,0:T(8,128)(2,1)S(1)}, bf16[14,1,768,128]{3,2,1,0:T(8,128)(2,1)S(1)}) fusion(pred[14,768]{1,0:T(8,128)(4,1)S(1)} %get-tuple-element.25, pred[14,768]{1,0:T(8,128)(4,1)S(1)} %get-tuple-element.10, bf16[14,2,768,128]{3,2,1,0:T(8,128)(2,1)} %broadcast_select_fusion, ...), kind=kLoop, calls=%fused_computation.25 | loop fusion | flops 5505024 | bytes 11045888 | tf_op jit(solution)/shard_map/jit(_where)/select_n | solution.py:56
  320.6 2.9 pad_maximum_fusion
  323.6 54.7 %all-reduce.5.cloned.1.call-done = f32[14,5120]{1,0:T(8,128)} async-done(((f32[14,5120]{1,0:T(8,128)}), f32[14,5120]{1,0:T(8,128)}) %all-reduce.5.cloned.1.call-update) | async-done | bytes 286736 | tf_op jit(solution)/shard_map/psum | solution.py:39
  378.3 1.7 fusion.86
  380.0 86.6 %reduce-scatter.2.cloned.1.call-done = bf16[56,5120]{1,0:T(8,128)(2,1)} async-done(((bf16[448,5120]{1,0:T(8,128)(2,1)}), bf16[56,5120]{1,0:T(8,128)(2,1)}) %reduce-scatter.2.cloned.1.call-update) | async-done | bytes 573456 | tf_op jit(solution)/shard_map/reduce_scatter | solution.py:191
  466.5 2.0 add_convert_fusion
  (101 shorter events, 3.1 us)
Async XLA Ops:
  7.2 2.0 copy-start
  11.9 19.2 %all-to-all-start = ((bf16[16,2,2560]{2,1,0:T(2,128)(2,1)}), bf16[16,2,2560]{2,1,0:T(2,128)(2,1)S(1)}, u32[]{:S(2)}, u32[]{:S(2)}) async-start(bf16[16,2,2560]{2,1,0:T(2,128)(2,1)} %reshape.612), calls=%async_computation | async-start | bytes 327680 | tf_op jit(solution)/shard_map/all_to_all | solution.py:149
  31.1 6.0 %copy-start.7 = (s32[224]{0:T(256)S(1)}, s32[224]{0:T(256)}, u32[]{:S(2)}) copy-start(s32[224]{0:T(256)} %param.16) | copy-start | bytes 2692
  31.1 6.8 %copy-start.9 = (s32[224]{0:T(256)S(1)}, s32[224]{0:T(256)}, u32[]{:S(2)}) copy-start(s32[224]{0:T(256)} %param.17) | copy-start | bytes 2692
  31.1 6.8 %copy-start.10 = (s32[224]{0:T(256)S(1)}, s32[224]{0:T(256)}, u32[]{:S(2)}) copy-start(s32[224]{0:T(256)} %param.15) | copy-start | bytes 2692
  31.1 8.1 %copy-start.5 = (f32[5120]{0:T(1024)S(1)}, f32[5120]{0:T(1024)}, u32[]{:S(2)}) copy-start(f32[5120]{0:T(1024)} %param.20) | copy-start | bytes 61444
  31.2 78.8 %all-to-all-start.1 = ((bf16[16,1,2,768,128]{4,3,2,1,0:T(8,128)(2,1)}), bf16[16,1,2,768,128]{4,3,2,1,0:T(8,128)(2,1)}, u32[]{:S(2)}, u32[]{:S(2)}) async-start(bf16[16,1,2,768,128]{4,3,2,1,0:T(8,128)(2,1)} %fusion.4), calls=%async_computation.1 | async-start | bytes 12582912 | tf_op jit(solution)/shard_map/all_to_all | solution.py:148
  37.1 181.0 %all-reduce.3.cloned.1.call-start = ((), (), s32[]{:S(2)}) async-start(), calls=%async_computation.3 | async-start | bytes 655360 | tf_op jit(solution)/shard_map/psum | solution.py:39
  39.3 5.8 %copy-start.8 = (f32[128]{0:T(128)S(1)}, f32[128]{0:T(128)}, u32[]{:S(2)}) copy-start(f32[128]{0:T(128)} %param.22) | copy-start | bytes 1540
  116.5 5.6 %copy-start.11 = (f32[128]{0:T(128)S(1)}, f32[128]{0:T(128)}, u32[]{:S(2)}) copy-start(f32[128]{0:T(128)} %param.21) | copy-start | bytes 1540
  129.5 4.9 %copy-start.6 = (s32[1,448]{1,0:T(1,128)S(1)}, s32[1,448]{1,0:T(1,128)}, u32[]{:S(2)}) copy-start(s32[1,448]{1,0:T(1,128)} %param.19) | copy-start | bytes 5380
  133.6 159.4 %all-gather.2.cloned.1.call-start = ((), (), s32[]{:S(2)}) async-start(), calls=%async_computation.5 | async-start | bytes 5160960 | tf_op jit(solution)/shard_map/all_gather | solution.py:169
  134.4 243.9 %all-reduce.5.cloned.1.call-start = ((), (), s32[]{:S(2)}) async-start(), calls=%async_computation.4 | async-start | bytes 655360 | tf_op jit(solution)/shard_map/psum | solution.py:39
  225.1 13.8 %slice-start.2 = ((s8[5242880]{0:T(1024)(128)(4,1)}), s8[1048576]{0:T(1024)(128)(4,1)S(1)}, s32[]{:S(2)}) async-start(s8[5242880]{0:T(1024)(128)(4,1)} %bitcast.143), calls=%async_computation.9 | async-start | bytes 2097152
  232.3 6.6 %slice-start.3 = ((s8[5242880]{0:T(1024)(128)(4,1)}), s8[4194304]{0:T(1024)(128)(4,1)S(1)}, s32[]{:S(2)}) async-start(s8[5242880]{0:T(1024)(128)(4,1)} %bitcast.143), calls=%async_computation.10 | async-start | bytes 8388608
  240.5 226.0 %reduce-scatter.2.cloned.1.call-start = ((), (), s32[]{:S(2)}) async-start(), calls=%async_computation.6 | async-start | bytes 5160960 | tf_op jit(solution)/shard_map/reduce_scatter | solution.py:191
  293.0 9.1 %slice-start = ((s8[5242880]{0:T(1024)(128)(4,1)}), s8[4194304]{0:T(1024)(128)(4,1)S(1)}, s32[]{:S(2)}) async-start(s8[5242880]{0:T(1024)(128)(4,1)} %bitcast.141), calls=%async_computation.7 | async-start | bytes 8388608
  293.0 9.1 %slice-start.6 = ((s8[4587520]{0:T(1024)(128)(4,1)}), s8[4194304]{0:T(1024)(128)(4,1)S(1)}, s32[]{:S(2)}) async-start(s8[4587520]{0:T(1024)(128)(4,1)} %bitcast.148), calls=%async_computation.13 | async-start | bytes 8388608
  296.4 5.7 %slice-start.1 = ((s8[5242880]{0:T(1024)(128)(4,1)}), s8[1048576]{0:T(1024)(128)(4,1)S(1)}, s32[]{:S(2)}) async-start(s8[5242880]{0:T(1024)(128)(4,1)} %bitcast.141), calls=%async_computation.8 | async-start | bytes 2097152
  296.4 5.7 %slice-start.7 = ((s8[4587520]{0:T(1024)(128)(4,1)}), s8[393216]{0:T(1024)(128)(4,1)S(1)}, s32[]{:S(2)}) async-start(s8[4587520]{0:T(1024)(128)(4,1)} %bitcast.148), calls=%async_computation.14 | async-start | bytes 786432
  301.3 0.8 copy-start.3
  306.1 2.8 copy-start.4
  308.1 2.6 slice-start.4
  308.9 1.9 slice-start.5
  320.6 145.9 %copy-start.2 = (bf16[56,5120]{1,0:T(8,128)(2,1)S(1)}, bf16[56,5120]{1,0:T(8,128)(2,1)}, u32[]{:S(2)}) copy-start(bf16[56,5120]{1,0:T(8,128)(2,1)} %param.18) | copy-start | bytes 1720324
  320.6 147.9 %copy-start.1 = (bf16[14,5120]{1,0:T(8,128)(2,1)S(1)}, bf16[14,5120]{1,0:T(8,128)(2,1)}, u32[]{:S(2)}) copy-start(bf16[14,5120]{1,0:T(8,128)(2,1)} %param.13) | copy-start | bytes 430084
Sparse Core Ops, SparseCore 0:
  133.7 84.2 all-reduce.2
  220.6 72.3 all-gather.1
  295.6 82.6 all-reduce.4
  382.0 84.4 reduce-scatter.1
where the time goes:
time: 476 us; the launch traced here: 475 us
  waiting for transfers between devices  342 us (72%)
  matrix products  53 us (11%)
  other arithmetic  33.5 us (7%)
  local copies, waits for them, and re-layouts  19.2 us (4%)
  between operations  14.3 us (3%)
  starting transfers between devices  12.7 us (3%)
    psum x2, waiting for transfers between devices, residual_update(): summed = lax.psum(partial_value, 'tp')  138 us
    reduce_scatter x1, waiting for transfers between devices, per_device(): lax.psum_scatter(jnp.dot(attn, w_out, preferred_element_type=jnp.float32)...  86.6 us
    all_to_all x1, waiting for transfers between devices, per_device(): lax.all_to_all(send_cache, 'group', split_axis=0, concat_axis=0, tiled=True)  64.7 us
    all_gather x1, waiting for transfers between devices, per_device(): lax.all_gather(score_rows, 'tp', axis=0, tiled=True)  52.2 us
    sub x2, matrix products, softmax_rows(): expo = jnp.exp(scores - top)  10.7 us
    dot_general x2, matrix products, decode_steps(): jnp.einsum('nkgc,nckd->nkgd', weights, vals.reshape(count, ctx, kv_local,...  10.5 us
  transfers between devices with their start and end apart: 6, of which 5 were waited for; matrix products, arithmetic and copies ran while one was open for 16% of the time, Pallas kernels for 0%

commit v1 on v0

v1 whole, which is shorter than its diff:
```python
import functools
import math

import jax
import jax.numpy as jnp
from jax import lax
from jax.experimental import pallas as pl
from jax.experimental.pallas import tpu as pltpu
from jax.sharding import PartitionSpec as P

HD = 128
EPS = 1e-06
MESH = pl.DeviceIdType.MESH
BF = jnp.bfloat16
F32 = jnp.float32
LOW = -1e30
INV = 1.0 / math.sqrt(HD)

D = 5120
CTX = 768
NG = 16
NT = 8
R = 14
RP = 16
SH = 56
SP = 64
TOK = NT * SP
HALF = D // 2
QUART = D // 4
SL = D // NT
MSG = SL + 4 * HD


def head_norm(vectors, gain):
    mean = jnp.mean(vectors * vectors, axis=-1, keepdims=True)
    return (vectors * lax.rsqrt(mean + EPS) * gain).astype(BF)


def dot(a, b):
    return jnp.dot(a, b, preferred_element_type=F32)


def dot_t(a, b):
    return lax.dot_general(a, b, (((1,), (1,)), ((), ())), preferred_element_type=F32)


def main_kernel(
    dest_ref, slot_ref, len_ref,
    dec_ref, score_ref, gain_ref, qgain_ref, kgain_ref, doc_ref,
    cache_hbm, wq_hbm, wkv_hbm, wo_hbm,
    got_ref, patch_ref, plan_ref, dec_out_ref, score_out_ref,
    cache, wkv, wqkv, wo, xin, docr_ref, docc_ref, packed, xg, xn, sc, qs, kt, vs, terms,
    relay, arrive, cross, score_sum, part, gather_part, xbuf, nx, scores, pick, fin, obuf,
    load_sem, a2a_send, a2a_recv, ag_send, ag_recv, rs_send, rs_recv,
    dp_send, dp_recv, dx_send, dx_recv, fin_send, fin_recv, o_send, o_recv,
):
    g = lax.axis_index("group")
    t = lax.axis_index("tp")
    y, h = t // 2, t % 2
    z, xl, core = g // 4, (g // 2) % 2, g % 2
    oh = 1 - h
    up, down, far = (y + 1) % 4, (y + 3) % 4, (y + 2) % 4
    mine, partner = t, y * 2 + oh
    to_up, to_down, to_x = {"tp": up * 2 + h}, {"tp": down * 2 + h}, {"tp": partner}

    def remote(src, dst, send, recv, device):
        return pltpu.make_async_remote_copy(
            src_ref=src, dst_ref=dst, send_sem=send, recv_sem=recv,
            device_id=device, device_id_type=MESH,
        )

    loads = [
        pltpu.make_async_copy(cache_hbm, cache, load_sem.at[0]),
        pltpu.make_async_copy(wq_hbm, wqkv.at[:, pl.ds(0, 512)], load_sem.at[1]),
        pltpu.make_async_copy(wkv_hbm, wkv, load_sem.at[2]),
        pltpu.make_async_copy(wo_hbm, wo, load_sem.at[3]),
    ]
    for load in loads:
        load.start()

    barrier = pltpu.get_barrier_semaphore()

    def greet_tp(k, c):
        pl.semaphore_signal(barrier, inc=1, device_id={"tp": (t + k) % NT}, device_id_type=MESH)
        return c

    def greet_group(k, c):
        pl.semaphore_signal(barrier, inc=1, device_id={"group": (g + k) % NG}, device_id_type=MESH)
        return c

    lax.fori_loop(1, NT, greet_tp, 0)
    lax.fori_loop(1, NG, greet_group, 0)

    for a in range(2):
        lo = score_ref[:, a * HALF : a * HALF + QUART].astype(F32)
        hi = score_ref[:, a * HALF + QUART : (a + 1) * HALF].astype(F32)
        xg[mine, a] = jnp.concatenate([lo, hi], axis=0).astype(BF)

    xin[...] = jnp.zeros_like(xin)
    xin[0:R, :] = dec_ref[...].astype(F32)
    token = lax.broadcasted_iota(jnp.int32, (TOK, NT * SH), 1)
    place = lax.broadcasted_iota(jnp.int32, (TOK, NT * SH), 0)
    inside = (place & (SP - 1)) < SH
    spread = ((place - (place >> 6) * (SP - SH) == token) & inside).astype(F32).astype(BF)
    ids = jnp.broadcast_to(doc_ref[...].astype(F32) + 1.0, (HD, NT * SH)).astype(BF)
    docr_ref[...] = dot_t(ids[:16], spread)
    docc_ref[...] = dot_t(spread, ids)

    lane = lax.broadcasted_iota(jnp.int32, (RP, NG * RP), 1)
    slot_row = lax.broadcasted_iota(jnp.int32, (RP, NG * RP), 0)

    def wanted(e, c):
        want, span = c
        for r in range(R):
            here = jnp.where(dest_ref[e * R + r] == g, slot_ref[e * R + r], -1)
            spot = lane == e * RP + r
            want = jnp.where(spot, here, want)
            span = jnp.where(spot, len_ref[e * R + r], span)
        return want, span

    none = jnp.full((RP, NG * RP), -1, jnp.int32)
    want, span = lax.fori_loop(0, NG, wanted, (none, jnp.zeros_like(none)))
    pick[...] = (want == slot_row).astype(F32).astype(BF)
    source = jnp.sum(jnp.where(want == slot_row, lane >> 4, 0), axis=-1, keepdims=True)
    length = jnp.sum(jnp.where(want == slot_row, span, 0), axis=-1, keepdims=True)
    plan_lane = lax.broadcasted_iota(jnp.int32, (RP, HD), 1)
    plan_ref[...] = jnp.where(plan_lane == 0, source, length)

    pl.semaphore_wait(barrier, NT - 1 + NG - 1)

    def ag(i, shard, a, device):
        where = xg.at[shard, a]
        return remote(where, where, ag_send.at[i], ag_recv.at[i], device)

    first = [ag(a, mine, a, to_up) for a in range(2)]
    first += [ag(2 + a, mine, a, to_down) for a in range(2)]
    first += [ag(4 + a, mine, a, to_x) for a in range(2)]
    for c in (first[4], first[0], first[3], first[1], first[2]):
        c.start()
    second = [ag(6 + a, partner, a, to_up) for a in range(2)]
    second += [ag(8 + a, partner, a, to_down) for a in range(2)]
    fwd_up = [ag(10, down * 2 + h, 0, to_up), ag(12, down * 2 + oh, 0, to_up)]
    fwd_down = [ag(11, up * 2 + h, 1, to_down), ag(13, up * 2 + oh, 1, to_down)]

    def a2a(j):
        dz, dx, dc = j // 4, (j // 2) % 2, j % 2
        target = ((z + dz) % 4) * 4 + ((xl + dx) % 2) * 2 + (core + dc) % 2
        copy = remote(packed.at[j], got_ref.at[g], a2a_send.at[j], a2a_recv.at[j], {"group": target})
        return target, copy

    def fill(j, target):
        row = 0
        for r in range(1, R):
            row = jnp.where(dest_ref[g * R + r] == target, r, row)
        for kv in range(2):
            packed[j, kv] = cache[row, kv]

    def send_cache(dx, i):
        j = (i // 2) * 4 + dx * 2 + i % 2
        target, copy = a2a(j)
        fill(j, target)
        copy.start()

    loads[0].wait()
    send_cache(1, 0)
    send_cache(0, 1)
    fill(0, g)
    own_copy = pltpu.make_async_copy(packed.at[0], got_ref.at[g], a2a_send.at[0])
    own_copy.start()

    row_of = lax.broadcasted_iota(jnp.int32, (4 * RP, HD), 0) & (RP - 1)
    column_row = lax.broadcasted_iota(jnp.int32, (HD, 4 * RP), 1) & (RP - 1)
    lens = jnp.ones((4 * RP, HD), jnp.int32)
    for r in range(R):
        lens = jnp.where(row_of == r, len_ref[g * R + r], lens)
    cached = lax.broadcasted_iota(jnp.int32, (4 * RP, CTX), 1) < lens[:, 0:1]

    def stack4(v):
        return jnp.concatenate([v] * 4, axis=0)

    def dec_project(step, x):
        wide = x.astype(F32)
        scale = lax.rsqrt(jnp.mean(wide * wide, axis=-1, keepdims=True) + EPS)
        nx[...] = (wide * gain_ref[...]).astype(BF)

        def chunk(k, acc):
            cols = pl.ds(pl.multiple_of(k * 1024, 1024), 1024)
            return acc + dot(nx[:, cols], wqkv[cols, :])

        proj = lax.fori_loop(0, 5, chunk, jnp.zeros((RP, 768), F32)) * scale
        q = jnp.concatenate([proj[:, i * HD : (i + 1) * HD] for i in range(4)], axis=0)
        q = head_norm(q, qgain_ref[...])
        return q, (head_norm(proj[:, 512:640], kgain_ref[...]), proj[:, 640:768].astype(BF))

    def dec_weights(q, new):
        qf = q.astype(F32)
        qt = qf.T.astype(BF)

        def chunk(n, c):
            spots = pl.ds(pl.multiple_of(n * HD, HD), HD)
            acc = jnp.zeros((HD, 4 * RP), F32)
            for r in range(R):
                acc = jnp.where(column_row == r, dot(cache[r, 0, spots, :], qt), acc)
            scores[:, spots] = acc.T
            return c

        lax.fori_loop(0, CTX // HD, chunk, 0)
        s = jnp.where(cached, scores[...] * INV, LOW)
        fresh = [
            jnp.sum(qf * stack4(k.astype(F32)), axis=-1, keepdims=True) * INV for k, _ in new
        ]
        top = functools.reduce(jnp.maximum, fresh, jnp.max(s, axis=-1, keepdims=True))
        e = jnp.exp(s - top)
        ef = [jnp.exp(f - top) for f in fresh]
        total = functools.reduce(jnp.add, ef, jnp.sum(e, axis=-1, keepdims=True))
        inv = 1.0 / total
        return (e * inv).astype(BF), [(f * inv).astype(BF).astype(F32) for f in ef]

    def dec_out(step, w, wf, new):
        def value_row(r, acc):
            return acc + jnp.where(row_of == r, dot(w, cache[r, 1]), 0.0)

        o = lax.fori_loop(0, R, value_row, jnp.zeros((4 * RP, HD), F32), unroll=True)
        for f, (_, v) in zip(wf, new):
            o = o + f * stack4(v.astype(F32))
        o = o.astype(BF)
        o = jnp.concatenate([o[i * RP : (i + 1) * RP] for i in range(4)], axis=1)

        def out_slice(p, c):
            part[step, p] = dot(o, wo[:, pl.ds(pl.multiple_of(p * SL, SL), SL)])
            return c

        lax.fori_loop(0, NT, out_slice, 0)
        lax.fori_loop(1, NT, lambda k, c: (part_copy(step, k).start(), c)[1], 0)

    def part_copy(step, k):
        peer = (t + k) % NT
        return remote(
            part.at[step, peer], gather_part.at[step, t],
            dp_send.at[step, k], dp_recv.at[step, k], {"tp": peer},
        )

    def reduce_parts(step, base):
        lax.fori_loop(1, NT, lambda k, c: (part_copy(step, k).wait_recv(), c)[1], 0)
        total = lax.fori_loop(
            1, NT, lambda k, acc: acc + gather_part[step, (t + k) % NT], part[step, t]
        )
        return (base.astype(F32) + total).astype(BF)

    def x_copy(k):
        return remote(xbuf.at[t], xbuf.at[t], dx_send.at[k], dx_recv.at[k], {"tp": (t + k) % NT})

    loads[2].wait()
    to_row = lax.broadcasted_iota(jnp.int32, (256, 256), 0)
    from_row = lax.broadcasted_iota(jnp.int32, (256, 256), 1)
    parting = (from_row == 2 * (to_row & (HD - 1)) + (to_row >= HD).astype(jnp.int32)).astype(F32).astype(BF)

    def part_rows(b, c):
        both = dot(parting, wkv[pl.ds(pl.multiple_of(b * 256, 256), 256), :]).astype(BF)
        rows = pl.ds(pl.multiple_of(b * HD, HD), HD)
        wqkv[rows, 512:640] = both[:HD]
        wqkv[rows, 640:768] = both[HD:]
        return c

    lax.fori_loop(0, D // HD, part_rows, 0, unroll=8)

    def prepare(p, c):
        total = jnp.zeros((SH, 1), F32)
        rows = pl.ds(pl.multiple_of(p * SP, SP), SP)
        for a in range(2):
            both = xg[p, a].astype(F32)
            for i in range(2):
                x = both[i * SH : (i + 1) * SH]
                total = total + jnp.sum(x * x, axis=-1, keepdims=True)
                start = a * HALF + i * QUART
                n = x * gain_ref[:, start : start + QUART]
                n = jnp.concatenate([n, jnp.zeros((SP - SH, QUART), F32)], axis=0)
                xn[rows, start : start + QUART] = n.astype(BF)
        scale = lax.rsqrt(total / D + EPS)
        scale = jnp.concatenate([scale, jnp.zeros((SP - SH, 1), F32)], axis=0)
        sc[rows, :] = jnp.broadcast_to(scale, (SP, HD))
        return c

    def project(block):
        rows = pl.ds(pl.multiple_of(block * 2 * SP, 2 * SP), 2 * SP)

        def tile(j):
            return dot(xn[rows, :], wqkv[:, j * 256 : (j + 1) * 256]) * sc[rows, 0:1]

        for j in range(2):
            v = tile(j)
            for i in range(2):
                qs[2 * j + i, rows, :] = head_norm(v[:, i * HD : (i + 1) * HD], qgain_ref[...])
        v = tile(2)
        k = head_norm(v[:, :HD], kgain_ref[...])
        kt[:, rows] = k.astype(F32).T.astype(BF)
        vs[rows, :] = v[:, HD:].astype(BF)

    loads[1].wait()
    q0, new0 = dec_project(0, xin[...])
    first[4].wait_send()
    first[5].start()
    send_cache(0, 2)
    send_cache(1, 1)
    w0, wf0 = dec_weights(q0, [new0])
    first[4].wait_recv()
    second[0].start()
    second[2].start()
    first[0].wait_recv()
    fwd_up[0].start()
    first[3].wait_recv()
    fwd_down[0].start()
    send_cache(1, 2)
    send_cache(0, 3)
    loads[3].wait()
    dec_out(0, w0, wf0, [new0])
    first[5].wait_recv()
    second[3].start()
    second[1].start()
    prepare(mine, 0)
    prepare(partner, 0)
    project(y)
    send_cache(1, 3)
    send_cache(0, 4)
    second[0].wait_recv()
    fwd_up[1].start()
    second[3].wait_recv()
    fwd_down[1].start()

    base0 = xin[:, pl.ds(pl.multiple_of(t * SL, SL), SL)]
    xbuf[t] = reduce_parts(0, base0)
    lax.fori_loop(1, NT, lambda k, c: (x_copy(k).start(), c)[1], 0)

    first[1].wait_recv()
    prepare(down * 2 + h, 0)
    first[2].wait_recv()
    prepare(up * 2 + h, 0)
    send_cache(1, 4)
    send_cache(0, 5)
    second[1].wait_recv()
    prepare(down * 2 + oh, 0)
    project(down)
    lax.fori_loop(1, NT, lambda k, c: (x_copy(k).wait_recv(), c)[1], 0)
    q1, new1 = dec_project(1, jnp.concatenate([xbuf[p] for p in range(NT)], axis=1))
    second[2].wait_recv()
    prepare(up * 2 + oh, 0)
    project(up)
    send_cache(1, 5)
    send_cache(0, 6)
    w1, wf1 = dec_weights(q1, [new0, new1])
    fwd_up[0].wait_recv()
    fwd_down[0].wait_recv()
    prepare(far * 2 + h, 0)
    fwd_up[1].wait_recv()
    fwd_down[1].wait_recv()
    prepare(far * 2 + oh, 0)
    project(far)
    send_cache(1, 6)

    later_col = lax.broadcasted_iota(jnp.int32, (2 * SP, TOK), 1)
    later_row = lax.broadcasted_iota(jnp.int32, (2 * SP, TOK), 0)

    def attend(block):
        rows = pl.ds(pl.multiple_of(block * 2 * SP, 2 * SP), 2 * SP)
        live = (docc_ref[rows, 0:1] == docr_ref[0:1, :]) & (later_col <= later_row + block * (2 * SP))
        heads = []
        for i in range(4):
            s = jnp.where(live, dot(qs[i, rows, :], kt[...]) * INV, LOW)
            e = jnp.exp(s - jnp.max(s, axis=-1, keepdims=True))
            inv = 1.0 / jnp.sum(e, axis=-1, keepdims=True)
            heads.append(dot((e * inv).astype(BF), vs[...]).astype(BF))
        attn = jnp.concatenate(heads, axis=1)
        for a in range(2):
            def columns(j, c):
                start = pl.multiple_of(a * HALF + j * 640, 640)
                lo = dot(attn, wo[:, pl.ds(start, 640)])
                hi = dot(attn, wo[:, pl.ds(pl.multiple_of(start + QUART, 640), 640)])
                for i in range(2):
                    pair = [v[i * SP : i * SP + SH] for v in (lo, hi)]
                    cols = pl.ds(pl.multiple_of(j * 640, 640), 640)
                    terms[block * 2 + i, a, :, cols] = jnp.concatenate(pair, axis=0).astype(BF)
                return c

            lax.fori_loop(0, 2, columns, 0)

    order = (oh, h)

    def rs(n, src, dst, device):
        return remote(src, dst, rs_send.at[n], rs_recv.at[n], device)

    far_up = [rs(i, terms.at[far * 2 + order[i], 0], relay.at[0, i], to_up) for i in range(2)]
    far_down = [rs(2 + i, terms.at[far * 2 + order[i], 1], relay.at[1, i], to_down) for i in range(2)]
    near_up = [
        [rs(4 + 2 * i + a, terms.at[up * 2 + order[i], a], arrive.at[0, i, a], to_up) for a in range(2)]
        for i in range(2)
    ]
    near_down = [
        [rs(8 + 2 * i + a, terms.at[down * 2 + order[i], a], arrive.at[1, i, a], to_down) for a in range(2)]
        for i in range(2)
    ]
    over = [rs(12 + a, cross.at[0, a], cross.at[1, a], to_x) for a in range(2)]

    def relay_up(i):
        far_up[i].wait_recv()
        spot = up * 2 + order[i]
        terms[spot, 0] = (terms[spot, 0].astype(F32) + relay[0, i].astype(F32)).astype(BF)
        near_up[i][0].start()

    def relay_down(i):
        far_down[i].wait_recv()
        spot = down * 2 + order[i]
        terms[spot, 1] = (terms[spot, 1].astype(F32) + relay[1, i].astype(F32)).astype(BF)
        near_down[i][1].start()

    def summed(i, a):
        near_up[i][a].wait_recv()
        near_down[i][a].wait_recv()
        return (
            terms[y * 2 + order[i], a].astype(F32)
            + arrive[0, i, a].astype(F32)
            + arrive[1, i, a].astype(F32)
        )

    attend(far)
    far_up[0].start()
    far_down[0].start()
    attend(up)
    near_up[0][1].start()
    send_cache(1, 7)
    attend(down)
    near_down[0][0].start()
    relay_up(0)
    relay_down(0)
    far_up[1].start()
    far_down[1].start()
    dec_out(1, w1, wf1, [new0, new1])
    attend(y)
    send_cache(0, 7)

    near_up[0][1].wait_send()
    near_up[1][1].start()
    near_down[0][0].wait_send()
    near_down[1][0].start()
    relay_up(1)
    relay_down(1)

    mine_rows = pl.ds(pl.multiple_of(g * RP, RP), RP)
    fin[mine_rows, 0:SL] = reduce_parts(1, xbuf[t])
    for i, (k, v) in enumerate([new0, new1]):
        start = SL + 2 * i * HD
        fin[mine_rows, start : start + HD] = k
        fin[mine_rows, start + HD : start + 2 * HD] = v

    def fin_copy(k):
        where = fin.at[mine_rows]
        return remote(where, where, fin_send.at[k], fin_recv.at[k], {"group": (g + k) % NG})

    lax.fori_loop(1, NG, lambda k, c: (fin_copy(k).start(), c)[1], 0)

    for a in range(2):
        cross[0, a] = summed(0, a).astype(BF)
        over[a].start()

    for a in range(2):
        near = summed(1, a)
        for i in range(2):
            cols = slice(a * HALF + i * QUART, a * HALF + (i + 1) * QUART)
            add = near[i * SH : (i + 1) * SH]
            score_sum[:, cols] = score_ref[:, cols].astype(F32) + add

    lax.fori_loop(1, NG, lambda k, c: (fin_copy(k).wait_recv(), c)[1], 0)
    placed = dot(pick[...], fin[...])
    obuf[t] = placed[:, :SL].astype(BF)
    patch_ref[...] = placed[:, SL:]

    def o_copy(k):
        return remote(obuf.at[t], obuf.at[t], o_send.at[k], o_recv.at[k], {"tp": (t + k) % NT})

    lax.fori_loop(1, NT, lambda k, c: (o_copy(k).start(), c)[1], 0)

    for a in range(2):
        over[a].wait_recv()
        far_half = cross[1, a].astype(F32)
        for i in range(2):
            cols = slice(a * HALF + i * QUART, a * HALF + (i + 1) * QUART)
            add = far_half[i * SH : (i + 1) * SH]
            score_out_ref[:, cols] = (score_sum[:, cols] + add).astype(BF)

    lax.fori_loop(1, NT, lambda k, c: (o_copy(k).wait_recv(), c)[1], 0)
    for p in range(NT):
        dec_out_ref[:, p * SL : (p + 1) * SL] = obuf[p]

    def end_a2a(j, c):
        a2a(j)[1].wait()
        return c

    lax.fori_loop(1, NG, end_a2a, 0)
    own_copy.wait()
    ended = first[:4] + first[5:] + second + fwd_up + fwd_down + far_up + far_down + over
    ended += near_up[1] + near_down[1] + [near_up[0][0], near_down[0][1]]
    for c in ended:
        c.wait_send()

    def end_tp(k, c):
        part_copy(0, k).wait_send()
        part_copy(1, k).wait_send()
        x_copy(k).wait_send()
        o_copy(k).wait_send()
        return c

    lax.fori_loop(1, NT, end_tp, 0)
    lax.fori_loop(1, NG, lambda k, c: (fin_copy(k).wait_send(), c)[1], 0)


def place_kernel(
    plan_ref, patch_ref, dec_ref, got_hbm, score_hbm,
    dec_out_ref, cache_out, score_out, rows, score_rows, in_sem, out_sem, score_sem,
):
    score_in = pltpu.make_async_copy(score_hbm, score_rows, score_sem.at[0])
    score_end = pltpu.make_async_copy(score_rows, score_out, score_sem.at[1])
    score_in.start()

    def get(s, c):
        pltpu.make_async_copy(got_hbm.at[plan_ref[s, 0]], rows.at[s], in_sem.at[s]).start()
        return c

    lax.fori_loop(0, R, get, 0)
    dec_out_ref[...] = dec_ref[:R, :]
    score_in.wait()
    score_end.start()

    def put(s, c):
        pltpu.make_async_copy(got_hbm.at[0], rows.at[s], in_sem.at[s]).wait()
        entry = patch_ref[pl.ds(s, 1), :]
        for step in range(2):
            pos = plan_ref[s, 1] + step
            base = pl.multiple_of((pos // 16) * 16, 16)
            here = lax.broadcasted_iota(jnp.int32, (16, HD), 0) == pos - base
            for kv in range(2):
                start = (2 * step + kv) * HD
                old = rows[s, kv, pl.ds(base, 16), :].astype(F32)
                both = jnp.where(here, entry[:, start : start + HD], old)
                rows[s, kv, pl.ds(base, 16), :] = both.astype(BF)
        pltpu.make_async_copy(rows.at[s], cache_out.at[s], out_sem.at[s]).start()
        return c

    lax.fori_loop(0, R, put, 0)

    def end(s, c):
        pltpu.make_async_copy(rows.at[s], cache_out.at[s], out_sem.at[s]).wait()
        return c

    lax.fori_loop(0, R, end, 0)
    score_end.wait()


def per_device(
    dec_rows, kv_cache, lengths, dest_group, dest_slot, score_rows, doc_ids,
    norm_gain, query_gain, key_gain, w_query, w_keyval, w_out,
):
    smem = pl.BlockSpec(memory_space=pltpu.SMEM)
    vmem = pl.BlockSpec(memory_space=pltpu.VMEM)
    hbm = pl.BlockSpec(memory_space=pl.ANY)
    dma = pltpu.SemaphoreType.DMA
    got, patch, plan, dec_out16, score_sum = pl.pallas_call(
        main_kernel,
        name="decode_and_score",
        out_shape=(
            jax.ShapeDtypeStruct((NG, 2, CTX, HD), BF),
            jax.ShapeDtypeStruct((RP, 4 * HD), F32),
            jax.ShapeDtypeStruct((RP, HD), jnp.int32),
            jax.ShapeDtypeStruct((RP, D), BF),
            jax.ShapeDtypeStruct((SH, D), BF),
        ),
        in_specs=[smem] * 3 + [vmem] * 6 + [hbm] * 4,
        out_specs=(hbm, vmem, vmem, vmem, vmem),
        scratch_shapes=[
            pltpu.VMEM((R, 2, CTX, HD), BF),
            pltpu.VMEM((2 * D, HD), BF),
            pltpu.VMEM((D, 768), BF),
            pltpu.VMEM((512, D), BF),
            pltpu.VMEM((RP, D), F32),
            pltpu.VMEM((16, TOK), F32),
            pltpu.VMEM((TOK, HD), F32),
            pltpu.VMEM((NG, 2, CTX, HD), BF),
            pltpu.VMEM((NT, 2, 2 * SH, QUART), BF),
            pltpu.VMEM((TOK, D), BF),
            pltpu.VMEM((TOK, HD), F32),
            pltpu.VMEM((4, TOK, HD), BF),
            pltpu.VMEM((HD, TOK), BF),
            pltpu.VMEM((TOK, HD), BF),
            pltpu.VMEM((NT, 2, 2 * SH, QUART), BF),
            pltpu.VMEM((2, 2, 2 * SH, QUART), BF),
            pltpu.VMEM((2, 2, 2, 2 * SH, QUART), BF),
            pltpu.VMEM((2, 2, 2 * SH, QUART), BF),
            pltpu.VMEM((SH, D), F32),
            pltpu.VMEM((2, NT, RP, SL), F32),
            pltpu.VMEM((2, NT, RP, SL), F32),
            pltpu.VMEM((NT, RP, SL), BF),
            pltpu.VMEM((RP, D), BF),
            pltpu.VMEM((4 * RP, CTX), F32),
            pltpu.VMEM((RP, NG * RP), BF),
            pltpu.VMEM((NG * RP, MSG), BF),
            pltpu.VMEM((NT, RP, SL), BF),
            dma((4,)), dma((NG,)), dma((NG,)), dma((14,)), dma((14,)), dma((14,)), dma((14,)),
            dma((2, NT)), dma((2, NT)), dma((NT,)), dma((NT,)), dma((NG,)), dma((NG,)),
            dma((NT,)), dma((NT,)),
        ],
        compiler_params=pltpu.CompilerParams(
            collective_id=0, has_side_effects=True, vmem_limit_bytes=60 * 1024 * 1024
        ),
        cost_estimate=pl.CostEstimate(flops=8 * 10**9, bytes_accessed=30 * 10**6, transcendentals=10**6),
    )(
        dest_group, dest_slot, lengths, dec_rows, score_rows, norm_gain.reshape(1, D),
        query_gain.reshape(1, HD), key_gain.reshape(1, HD), doc_ids,
        kv_cache, w_query, w_keyval.reshape(2 * D, HD), w_out,
    )
    return pl.pallas_call(
        place_kernel,
        name="place_rows",
        out_shape=(
            jax.ShapeDtypeStruct((R, D), BF),
            jax.ShapeDtypeStruct((R, 2, CTX, HD), BF),
            jax.ShapeDtypeStruct((SH, D), BF),
        ),
        in_specs=[smem] + [vmem] * 2 + [hbm] * 2,
        out_specs=(vmem, hbm, hbm),
        scratch_shapes=[
            pltpu.VMEM((R, 2, CTX, HD), BF),
            pltpu.VMEM((SH, D), BF),
            dma((R,)), dma((R,)), dma((2,)),
        ],
        compiler_params=pltpu.CompilerParams(vmem_limit_bytes=60 * 1024 * 1024),
        cost_estimate=pl.CostEstimate(flops=10**6, bytes_accessed=12 * 10**6, transcendentals=0),
    )(plan, patch, dec_out16, got, score_sum)


def solution(mesh):
    placed = (
        P("group", None),
        P("group", None, None, "tp"),
        P(),
        P(),
        P(),
        P(("group", "tp"), None),
        P("group", None),
        P(),
        P(),
        P(),
        P(None, "tp"),
        P(None, None, "tp"),
        P("tp", None),
    )
    return jax.shard_map(
        per_device,
        mesh=mesh,
        in_specs=placed,
        out_specs=(P("group", None), P("group", None, None, "tp"), P(("group", "tp"), None)),
        check_vma=False,
    )
```

time: 476 us -> 138 us (0.29)
  waiting for transfers between devices: 342 us -> 0 us
  Pallas kernels: 0 us -> 136 us
  matrix products: 53 us -> 0 us
  other arithmetic: 33.5 us -> 0 us
  local copies, waits for them, and re-layouts: 19.2 us -> 0 us
  between operations: 14.3 us -> 0.8 us
  starting transfers between devices: 12.7 us -> 0 us
    psum x2 -> x0, waiting for transfers between devices: 138 us -> none  [residual_update(): summed = lax.psum(partial_value, 'tp')]
    pallas_call x0 -> x2, Pallas kernels: none -> 136 us  [the longest x1 129 us: per_device(): pl.pallas_call(main_kernel, name='decode_and_score', out_shape=(jax.Shape...]
    reduce_scatter x1 -> x0, waiting for transfers between devices: 86.6 us -> none  [per_device(): lax.psum_scatter(jnp.dot(attn, w_out, preferred_element_type=jnp.float32)...]
    all_to_all x2 -> x0, waiting for transfers between devices: 64.7 us -> none  [the longest x1 64.7 us: per_device(): lax.all_to_all(send_cache, 'group', split_axis=0, concat_axis=0, tiled=True)]
    all_gather x1 -> x0, waiting for transfers between devices: 52.2 us -> none  [per_device(): lax.all_gather(score_rows, 'tp', axis=0, tiled=True)]
    dot_general x13 -> x0, matrix products: 42.3 us -> none  [the longest x2 10.5 us: decode_steps(): jnp.einsum('nkgc,nckd->nkgd', weights, vals.reshape(count, ctx, kv_local,...]
    select_n x7 -> x0, other arithmetic: 17.8 us -> none  [the longest x1 6.19 us: pack_for_send(): jnp.where(filled[:, None, None, None], jnp.take(cache, picks, axis=0), jn...]
    gather x4 -> x0, local copies, waits for them, and re-layouts: 14.4 us -> none  [the longest x1 6.57 us: pack_for_send(): jnp.take(cache, picks, axis=0)]
  transfers between devices with their start and end apart: 6 -> 0, of which waited for: 5 -> 0; matrix products, arithmetic and copies ran while one was open for 16% -> 0% of each run, Pallas kernels for 0% -> 0%
where the time goes in v1:
time: 138 us; the launch traced here: 137 us
  Pallas kernels  136 us (99%)
    pallas_call x1, Pallas kernels, per_device(): pl.pallas_call(main_kernel, name='decode_and_score', out_shape=(jax.Shape...  129 us
    pallas_call x1, Pallas kernels, per_device(): pl.pallas_call(place_kernel, name='place_rows', out_shape=(jax.ShapeDtype...  7.09 us

profile of v1, /device:TPU:0, one launch (start us, length us, event | category | flops | bytes accessed | tf_op | source)
XLA Modules:
  0.0 136.8 jit_solution(2081420673667372686)
XLA Ops:
  0.6 128.9 %decode_and_score.1 = (bf16[16,2,768,128]{3,2,1,0:T(8,128)(2,1)}, f32[16,512]{1,0:T(8,128)}, s32[16,128]{1,0:T(8,128)}, bf16[16,5120]{1,0:T(8,128)(2,1)}, bf16[56,5120]{1,0:T(8,128)(2,1)}) custom-call(s32[224]{0:T(256)} %dest_ref.1, s32[224]{0:T(256)} %slot_ref.1, s32[224]{0:T(256)} %len_ref.1, bf16[14,5120]{1,0:T(8,128)(2,1)} %dec_ref.1, ...), custom_call_target="tpu_custom_call" | custom-call | flops 8000000000 | bytes 30000000 | tf_op jit(solution)/shard_map/decode_and_score/pallas_call | solution.py:565
  129.6 7.1 %place_rows.1 = (bf16[14,5120]{1,0:T(8,128)(2,1)}, bf16[14,2,768,128]{3,2,1,0:T(8,128)(2,1)}, bf16[56,5120]{1,0:T(8,128)(2,1)}) custom-call(s32[16,128]{1,0:T(8,128)} %get-tuple-element.8.plan_ref, f32[16,512]{1,0:T(8,128)} %get-tuple-element.9.patch_ref, bf16[16,5120]{1,0:T(8,128)(2,1)} %get-tuple-element.10.dec_ref, ...), custom_call_target="tpu_custom_call" | custom-call | flops 1000000 | bytes 12000000 | tf_op jit(solution)/shard_map/place_rows/pallas_call | solution.py:618

commit v2 on v1

--- a/solution.py
+++ b/solution.py
@@ -96,6 +96,46 @@
         hi = score_ref[:, a * HALF + QUART : (a + 1) * HALF].astype(F32)
         xg[mine, a] = jnp.concatenate([lo, hi], axis=0).astype(BF)
 
+    pl.semaphore_wait(barrier, NT - 1 + NG - 1)
+
+    def ag(i, where, device):
+        return remote(where, where, ag_send.at[i], ag_recv.at[i], device)
+
+    over_x = ag(0, xg.at[mine], to_x)
+    first_up, first_down = ag(1, xg.at[mine], to_up), ag(2, xg.at[mine], to_down)
+    for c in (over_x, first_up, first_down):
+        c.start()
+    second_up, second_down = ag(3, xg.at[partner], to_up), ag(4, xg.at[partner], to_down)
+    fwd_up = [ag(5 + i, xg.at[down * 2 + hh, 0], to_up) for i, hh in enumerate((h, oh))]
+    fwd_down = [ag(7 + i, xg.at[up * 2 + hh, 1], to_down) for i, hh in enumerate((h, oh))]
+
+    def a2a(j):
+        dz, dx, dc = j // 4, (j // 2) % 2, j % 2
+        target = ((z + dz) % 4) * 4 + ((xl + dx) % 2) * 2 + (core + dc) % 2
+        copy = remote(packed.at[j], got_ref.at[g], a2a_send.at[j], a2a_recv.at[j], {"group": target})
+        return target, copy
+
+    def fill(j, target):
+        row = 0
+        for r in range(1, R):
+            row = jnp.where(dest_ref[g * R + r] == target, r, row)
+        for kv in range(2):
+            packed[j, kv] = cache[row, kv]
+
+    def send_caches(along, across=()):
+        for dx, some in ((1, across), (0, along)):
+            for i in some:
+                j = (i // 2) * 4 + dx * 2 + i % 2
+                target, copy = a2a(j)
+                fill(j, target)
+                copy.start()
+
+    loads[0].wait()
+    send_caches((1, 2, 6))
+    fill(0, g)
+    own_copy = pltpu.make_async_copy(packed.at[0], got_ref.at[g], a2a_send.at[0])
+    own_copy.start()
+
     xin[...] = jnp.zeros_like(xin)
     xin[0:R, :] = dec_ref[...].astype(F32)
     token = lax.broadcasted_iota(jnp.int32, (TOK, NT * SH), 1)
@@ -125,48 +165,6 @@
     length = jnp.sum(jnp.where(want == slot_row, span, 0), axis=-1, keepdims=True)
     plan_lane = lax.broadcasted_iota(jnp.int32, (RP, HD), 1)
     plan_ref[...] = jnp.where(plan_lane == 0, source, length)
-
-    pl.semaphore_wait(barrier, NT - 1 + NG - 1)
-
-    def ag(i, shard, a, device):
-        where = xg.at[shard, a]
-        return remote(where, where, ag_send.at[i], ag_recv.at[i], device)
-
-    first = [ag(a, mine, a, to_up) for a in range(2)]
-    first += [ag(2 + a, mine, a, to_down) for a in range(2)]
-    first += [ag(4 + a, mine, a, to_x) for a in range(2)]
-    for c in (first[4], first[0], first[3], first[1], first[2]):
-        c.start()
-    second = [ag(6 + a, partner, a, to_up) for a in range(2)]
-    second += [ag(8 + a, partner, a, to_down) for a in range(2)]
-    fwd_up = [ag(10, down * 2 + h, 0, to_up), ag(12, down * 2 + oh, 0, to_up)]
-    fwd_down = [ag(11, up * 2 + h, 1, to_down), ag(13, up * 2 + oh, 1, to_down)]
-
-    def a2a(j):
-        dz, dx, dc = j // 4, (j // 2) % 2, j % 2
-        target = ((z + dz) % 4) * 4 + ((xl + dx) % 2) * 2 + (core + dc) % 2
-        copy = remote(packed.at[j], got_ref.at[g], a2a_send.at[j], a2a_recv.at[j], {"group": target})
-        return target, copy
-
-    def fill(j, target):
-        row = 0
-        for r in range(1, R):
-            row = jnp.where(dest_ref[g * R + r] == target, r, row)
-        for kv in range(2):
-            packed[j, kv] = cache[row, kv]
-
-    def send_cache(dx, i):
-        j = (i // 2) * 4 + dx * 2 + i % 2
-        target, copy = a2a(j)
-        fill(j, target)
-        copy.start()
-
-    loads[0].wait()
-    send_cache(1, 0)
-    send_cache(0, 1)
-    fill(0, g)
-    own_copy = pltpu.make_async_copy(packed.at[0], got_ref.at[g], a2a_send.at[0])
-    own_copy.start()
 
     row_of = lax.broadcasted_iota(jnp.int32, (4 * RP, HD), 0) & (RP - 1)
     column_row = lax.broadcasted_iota(jnp.int32, (HD, 4 * RP), 1) & (RP - 1)
@@ -298,56 +296,38 @@
 
     loads[1].wait()
     q0, new0 = dec_project(0, xin[...])
-    first[4].wait_send()
-    first[5].start()
-    send_cache(0, 2)
-    send_cache(1, 1)
+    over_x.wait_recv()
+    second_up.start()
+    second_down.start()
+    first_up.wait_recv()
+    fwd_up[0].start()
+    first_down.wait_recv()
+    fwd_down[0].start()
+    send_caches((3, 7), (0, 1))
     w0, wf0 = dec_weights(q0, [new0])
-    first[4].wait_recv()
-    second[0].start()
-    second[2].start()
-    first[0].wait_recv()
-    fwd_up[0].start()
-    first[3].wait_recv()
-    fwd_down[0].start()
-    send_cache(1, 2)
-    send_cache(0, 3)
     loads[3].wait()
     dec_out(0, w0, wf0, [new0])
-    first[5].wait_recv()
-    second[3].start()
-    second[1].start()
     prepare(mine, 0)
     prepare(partner, 0)
     project(y)
-    send_cache(1, 3)
-    send_cache(0, 4)
-    second[0].wait_recv()
-    fwd_up[1].start()
-    second[3].wait_recv()
-    fwd_down[1].start()
+    prepare(down * 2 + h, 0)
+    prepare(up * 2 + h, 0)
 
     base0 = xin[:, pl.ds(pl.multiple_of(t * SL, SL), SL)]
     xbuf[t] = reduce_parts(0, base0)
     lax.fori_loop(1, NT, lambda k, c: (x_copy(k).start(), c)[1], 0)
 
-    first[1].wait_recv()
-    prepare(down * 2 + h, 0)
-    first[2].wait_recv()
-    prepare(up * 2 + h, 0)
-    send_cache(1, 4)
-    send_cache(0, 5)
-    second[1].wait_recv()
+    second_up.wait_recv()
+    fwd_up[1].start()
+    second_down.wait_recv()
+    fwd_down[1].start()
+    send_caches((4,), (2, 3))
     prepare(down * 2 + oh, 0)
     project(down)
+    prepare(up * 2 + oh, 0)
+    project(up)
     lax.fori_loop(1, NT, lambda k, c: (x_copy(k).wait_recv(), c)[1], 0)
     q1, new1 = dec_project(1, jnp.concatenate([xbuf[p] for p in range(NT)], axis=1))
-    second[2].wait_recv()
-    prepare(up * 2 + oh, 0)
-    project(up)
-    send_cache(1, 5)
-    send_cache(0, 6)
-    w1, wf1 = dec_weights(q1, [new0, new1])
     fwd_up[0].wait_recv()
     fwd_down[0].wait_recv()
     prepare(far * 2 + h, 0)
@@ -355,7 +335,7 @@
     fwd_down[1].wait_recv()
     prepare(far * 2 + oh, 0)
     project(far)
-    send_cache(1, 6)
+    send_caches((5,), (4, 5))
 
     later_col = lax.broadcasted_iota(jnp.int32, (2 * SP, TOK), 1)
     later_row = lax.broadcasted_iota(jnp.int32, (2 * SP, TOK), 0)
@@ -425,24 +405,24 @@
     far_up[0].start()
     far_down[0].start()
     attend(up)
+    attend(down)
+    far_up[0].wait_send()
     near_up[0][1].start()
-    send_cache(1, 7)
-    attend(down)
+    far_down[0].wait_send()
     near_down[0][0].start()
     relay_up(0)
     relay_down(0)
-    far_up[1].start()
-    far_down[1].start()
+    send_caches((), (6, 7))
+    w1, wf1 = dec_weights(q1, [new0, new1])
     dec_out(1, w1, wf1, [new0, new1])
     attend(y)
-    send_cache(0, 7)
-
-    near_up[0][1].wait_send()
-    near_up[1][1].start()
-    near_down[0][0].wait_send()
-    near_down[1][0].start()
-    relay_up(1)
-    relay_down(1)
+    near_up[0][0].wait_send()
+    far_up[1].start()
+    near_down[0][1].wait_send()
+    far_down[1].start()
+    for a in range(2):
+        cross[0, a] = summed(0, a).astype(BF)
+        over[a].start()
 
     mine_rows = pl.ds(pl.multiple_of(g * RP, RP), RP)
     fin[mine_rows, 0:SL] = reduce_parts(1, xbuf[t])
@@ -457,9 +437,12 @@
 
     lax.fori_loop(1, NG, lambda k, c: (fin_copy(k).start(), c)[1], 0)
 
-    for a in range(2):
-        cross[0, a] = summed(0, a).astype(BF)
-        over[a].start()
+    far_up[1].wait_send()
+    near_up[1][1].start()
+    far_down[1].wait_send()
+    near_down[1][0].start()
+    relay_up(1)
+    relay_down(1)
 
     for a in range(2):
         near = summed(1, a)
@@ -496,8 +479,8 @@
 
     lax.fori_loop(1, NG, end_a2a, 0)
     own_copy.wait()
-    ended = first[:4] + first[5:] + second + fwd_up + fwd_down + far_up + far_down + over
-    ended += near_up[1] + near_down[1] + [near_up[0][0], near_down[0][1]]
+    ended = [over_x, first_up, first_down, second_up, second_down] + fwd_up + fwd_down + over
+    ended += near_up[1] + near_down[1] + [near_up[0][1], near_down[0][0]]
     for c in ended:
         c.wait_send()
 
@@ -602,7 +585,7 @@
             pltpu.VMEM((RP, NG * RP), BF),
             pltpu.VMEM((NG * RP, MSG), BF),
             pltpu.VMEM((NT, RP, SL), BF),
-            dma((4,)), dma((NG,)), dma((NG,)), dma((14,)), dma((14,)), dma((14,)), dma((14,)),
+            dma((4,)), dma((NG,)), dma((NG,)), dma((9,)), dma((9,)), dma((14,)), dma((14,)),
             dma((2, NT)), dma((2, NT)), dma((NT,)), dma((NT,)), dma((NG,)), dma((NG,)),
             dma((NT,)), dma((NT,)),
         ],

time: 138 us -> 139 us (level)
  Pallas kernels: 136 us -> 138 us
    pallas_call x1, Pallas kernels: 129 us -> 131 us  [per_device(): pl.pallas_call(main_kernel, name='decode_and_score', out_shape=(jax.Shape...]
where the time goes in v2:
time: 139 us
  Pallas kernels  138 us (99%)
    pallas_call x1, Pallas kernels, per_device(): pl.pallas_call(main_kernel, name='decode_and_score', out_shape=(jax.Shape...  131 us
    pallas_call x1, Pallas kernels, per_device(): pl.pallas_call(place_kernel, name='place_rows', out_shape=(jax.ShapeDtype...  7.09 us

profile of v2, /device:TPU:0, one launch (start us, length us, event | category | flops | bytes accessed | tf_op | source)
XLA Modules:
  0.0 139.2 jit_solution(17380148882511703863)
XLA Ops:
  0.6 131.3 %decode_and_score.1 = (bf16[16,2,768,128]{3,2,1,0:T(8,128)(2,1)}, f32[16,512]{1,0:T(8,128)}, s32[16,128]{1,0:T(8,128)}, bf16[16,5120]{1,0:T(8,128)(2,1)}, bf16[56,5120]{1,0:T(8,128)(2,1)}) custom-call(s32[224]{0:T(256)} %dest_ref.1, s32[224]{0:T(256)} %slot_ref.1, s32[224]{0:T(256)} %len_ref.1, bf16[14,5120]{1,0:T(8,128)(2,1)} %dec_ref.1, ...), custom_call_target="tpu_custom_call" | custom-call | flops 8000000000 | bytes 30000000 | tf_op jit(solution)/shard_map/decode_and_score/pallas_call | solution.py:548
  131.9 7.1 %place_rows.1 = (bf16[14,5120]{1,0:T(8,128)(2,1)}, bf16[14,2,768,128]{3,2,1,0:T(8,128)(2,1)}, bf16[56,5120]{1,0:T(8,128)(2,1)}) custom-call(s32[16,128]{1,0:T(8,128)} %get-tuple-element.8.plan_ref, f32[16,512]{1,0:T(8,128)} %get-tuple-element.9.patch_ref, bf16[16,5120]{1,0:T(8,128)(2,1)} %get-tuple-element.10.dec_ref, ...), custom_call_target="tpu_custom_call" | custom-call | flops 1000000 | bytes 12000000 | tf_op jit(solution)/shard_map/place_rows/pallas_call | solution.py:601

commit v3 on v2

--- a/solution.py
+++ b/solution.py
@@ -29,6 +29,8 @@
 QUART = D // 4
 SL = D // NT
 MSG = SL + 4 * HD
+GATHER_CUTS = ((0, 64), (64, 48))
+SUM_CUTS = ((0, 48), (48, 32), (80, 32))
 
 
 def head_norm(vectors, gain):
@@ -38,6 +40,23 @@
 
 def dot(a, b):
     return jnp.dot(a, b, preferred_element_type=F32)
+
+
+class Several:
+    def __init__(self, copies):
+        self.copies = copies
+
+    def start(self):
+        for copy in self.copies:
+            copy.start()
+
+    def wait_recv(self):
+        for copy in self.copies:
+            copy.wait_recv()
+
+    def wait_send(self):
+        for copy in self.copies:
+            copy.wait_send()
 
 
 def dot_t(a, b):
@@ -98,16 +117,29 @@
 
     pl.semaphore_wait(barrier, NT - 1 + NG - 1)
 
-    def ag(i, where, device):
-        return remote(where, where, ag_send.at[i], ag_recv.at[i], device)
-
-    over_x = ag(0, xg.at[mine], to_x)
-    first_up, first_down = ag(1, xg.at[mine], to_up), ag(2, xg.at[mine], to_down)
+    def pieces(cuts, src, dst, send, recv, base, device):
+        return [
+            remote(
+                src.at[pl.ds(lo, n), :], dst.at[pl.ds(lo, n), :],
+                send.at[base + i], recv.at[base + i], device,
+            )
+            for i, (lo, n) in enumerate(cuts)
+        ]
+
+    def ag(base, shard, halves, device):
+        copies = []
+        for i, a in enumerate(halves):
+            where = xg.at[shard, a]
+            copies += pieces(GATHER_CUTS, where, where, ag_send, ag_recv, base + 2 * i, device)
+        return Several(copies)
+
+    over_x = ag(0, mine, (0, 1), to_x)
+    first_up, first_down = ag(4, mine, (0, 1), to_up), ag(8, mine, (0, 1), to_down)
     for c in (over_x, first_up, first_down):
         c.start()
-    second_up, second_down = ag(3, xg.at[partner], to_up), ag(4, xg.at[partner], to_down)
-    fwd_up = [ag(5 + i, xg.at[down * 2 + hh, 0], to_up) for i, hh in enumerate((h, oh))]
-    fwd_down = [ag(7 + i, xg.at[up * 2 + hh, 1], to_down) for i, hh in enumerate((h, oh))]
+    second_up, second_down = ag(12, partner, (0, 1), to_up), ag(16, partner, (0, 1), to_down)
+    fwd_up = [ag(20 + 2 * i, down * 2 + hh, (0,), to_up) for i, hh in enumerate((h, oh))]
+    fwd_down = [ag(24 + 2 * i, up * 2 + hh, (1,), to_down) for i, hh in enumerate((h, oh))]
 
     def a2a(j):
         dz, dx, dc = j // 4, (j // 2) % 2, j % 2
@@ -351,22 +383,17 @@
             heads.append(dot((e * inv).astype(BF), vs[...]).astype(BF))
         attn = jnp.concatenate(heads, axis=1)
         for a in range(2):
-            def columns(j, c):
-                start = pl.multiple_of(a * HALF + j * 640, 640)
-                lo = dot(attn, wo[:, pl.ds(start, 640)])
-                hi = dot(attn, wo[:, pl.ds(pl.multiple_of(start + QUART, 640), 640)])
-                for i in range(2):
-                    pair = [v[i * SP : i * SP + SH] for v in (lo, hi)]
-                    cols = pl.ds(pl.multiple_of(j * 640, 640), 640)
-                    terms[block * 2 + i, a, :, cols] = jnp.concatenate(pair, axis=0).astype(BF)
-                return c
-
-            lax.fori_loop(0, 2, columns, 0)
+            lo, hi = [
+                dot(attn, wo[:, a * HALF + i * QUART : a * HALF + (i + 1) * QUART]) for i in range(2)
+            ]
+            for i in range(2):
+                pair = [v[i * SP : i * SP + SH] for v in (lo, hi)]
+                terms[block * 2 + i, a] = jnp.concatenate(pair, axis=0).astype(BF)
 
     order = (oh, h)
 
     def rs(n, src, dst, device):
-        return remote(src, dst, rs_send.at[n], rs_recv.at[n], device)
+        return Several(pieces(SUM_CUTS, src, dst, rs_send, rs_recv, 3 * n, device))
 
     far_up = [rs(i, terms.at[far * 2 + order[i], 0], relay.at[0, i], to_up) for i in range(2)]
     far_down = [rs(2 + i, terms.at[far * 2 + order[i], 1], relay.at[1, i], to_down) for i in range(2)]
@@ -585,7 +612,7 @@
             pltpu.VMEM((RP, NG * RP), BF),
             pltpu.VMEM((NG * RP, MSG), BF),
             pltpu.VMEM((NT, RP, SL), BF),
-            dma((4,)), dma((NG,)), dma((NG,)), dma((9,)), dma((9,)), dma((14,)), dma((14,)),
+            dma((4,)), dma((NG,)), dma((NG,)), dma((28,)), dma((28,)), dma((42,)), dma((42,)),
             dma((2, NT)), dma((2, NT)), dma((NT,)), dma((NT,)), dma((NG,)), dma((NG,)),
             dma((NT,)), dma((NT,)),
         ],

time: 139 us -> 140 us (level)
  no operation moved by 1% of the time
where the time goes in v3:
time: 140 us
  Pallas kernels  139 us (99%)
    pallas_call x1, Pallas kernels, per_device(): pl.pallas_call(main_kernel, name='decode_and_score', out_shape=(jax.Shape...  132 us
    pallas_call x1, Pallas kernels, per_device(): pl.pallas_call(place_kernel, name='place_rows', out_shape=(jax.ShapeDtype...  7.09 us

profile of v3, /device:TPU:0, one launch (start us, length us, event | category | flops | bytes accessed | tf_op | source)
XLA Modules:
  0.0 140.1 jit_solution(13702157435266679313)
XLA Ops:
  0.6 132.2 %decode_and_score.1 = (bf16[16,2,768,128]{3,2,1,0:T(8,128)(2,1)}, f32[16,512]{1,0:T(8,128)}, s32[16,128]{1,0:T(8,128)}, bf16[16,5120]{1,0:T(8,128)(2,1)}, bf16[56,5120]{1,0:T(8,128)(2,1)}) custom-call(s32[224]{0:T(256)} %dest_ref.1, s32[224]{0:T(256)} %slot_ref.1, s32[224]{0:T(256)} %len_ref.1, bf16[14,5120]{1,0:T(8,128)(2,1)} %dec_ref.1, ...), custom_call_target="tpu_custom_call" | custom-call | flops 8000000000 | bytes 30000000 | tf_op jit(solution)/shard_map/decode_and_score/pallas_call | solution.py:575
  132.9 7.1 %place_rows.1 = (bf16[14,5120]{1,0:T(8,128)(2,1)}, bf16[14,2,768,128]{3,2,1,0:T(8,128)(2,1)}, bf16[56,5120]{1,0:T(8,128)(2,1)}) custom-call(s32[16,128]{1,0:T(8,128)} %get-tuple-element.8.plan_ref, f32[16,512]{1,0:T(8,128)} %get-tuple-element.9.patch_ref, bf16[16,5120]{1,0:T(8,128)(2,1)} %get-tuple-element.10.dec_ref, ...), custom_call_target="tpu_custom_call" | custom-call | flops 1000000 | bytes 12000000 | tf_op jit(solution)/shard_map/place_rows/pallas_call | solution.py:628

commit v4 on v3

--- a/solution.py
+++ b/solution.py
@@ -29,8 +29,8 @@
 QUART = D // 4
 SL = D // NT
 MSG = SL + 4 * HD
-GATHER_CUTS = ((0, 64), (64, 48))
-SUM_CUTS = ((0, 48), (48, 32), (80, 32))
+GATHER_CUTS = ((0, 112),)
+SUM_CUTS = ((0, 112),)
 
 
 def head_norm(vectors, gain):
@@ -69,8 +69,8 @@
     cache_hbm, wq_hbm, wkv_hbm, wo_hbm,
     got_ref, patch_ref, plan_ref, dec_out_ref, score_out_ref,
     cache, wkv, wqkv, wo, xin, docr_ref, docc_ref, packed, xg, xn, sc, qs, kt, vs, terms,
-    relay, arrive, cross, score_sum, part, gather_part, xbuf, nx, scores, pick, fin, obuf,
-    load_sem, a2a_send, a2a_recv, ag_send, ag_recv, rs_send, rs_recv,
+    relay, arrive, cross, through_x, through_z, through_cross, score_sum, part, gather_part, xbuf, nx, scores, pick, fin, obuf,
+    load_sem, a2a_send, a2a_recv, ex_send, ex_recv, zi_send, zi_recv, zo_send, zo_recv, ag_send, ag_recv, rs_send, rs_recv,
     dp_send, dp_recv, dx_send, dx_recv, fin_send, fin_recv, o_send, o_recv,
 ):
     g = lax.axis_index("group")
@@ -80,7 +80,9 @@
     oh = 1 - h
     up, down, far = (y + 1) % 4, (y + 3) % 4, (y + 2) % 4
     mine, partner = t, y * 2 + oh
-    to_up, to_down, to_x = {"tp": up * 2 + h}, {"tp": down * 2 + h}, {"tp": partner}
+    g_x = z * 4 + (1 - xl) * 2 + core
+    to_up, to_down = {"tp": up * 2 + h}, {"tp": down * 2 + h}
+    via_same, via_other = (g_x, t), (g_x, partner)
 
     def remote(src, dst, send, recv, device):
         return pltpu.make_async_remote_copy(
@@ -109,13 +111,14 @@
 
     lax.fori_loop(1, NT, greet_tp, 0)
     lax.fori_loop(1, NG, greet_group, 0)
+    pl.semaphore_signal(barrier, inc=1, device_id=(g_x, partner), device_id_type=MESH)
 
     for a in range(2):
         lo = score_ref[:, a * HALF : a * HALF + QUART].astype(F32)
         hi = score_ref[:, a * HALF + QUART : (a + 1) * HALF].astype(F32)
         xg[mine, a] = jnp.concatenate([lo, hi], axis=0).astype(BF)
 
-    pl.semaphore_wait(barrier, NT - 1 + NG - 1)
+    pl.semaphore_wait(barrier, NT + NG - 1)
 
     def pieces(cuts, src, dst, send, recv, base, device):
         return [
@@ -133,19 +136,34 @@
             copies += pieces(GATHER_CUTS, where, where, ag_send, ag_recv, base + 2 * i, device)
         return Several(copies)
 
-    over_x = ag(0, mine, (0, 1), to_x)
+    def exchange(src, through, dst, send, recv):
+        ins = [
+            remote(src.at[a], through.at[a], send.at[a], recv.at[a], device)
+            for a, device in enumerate((via_same, via_other))
+        ]
+        outs = [
+            remote(through.at[a], dst(a), send.at[2 + a], recv.at[2 + a], device)
+            for a, device in enumerate((via_other, via_same))
+        ]
+        return ins, outs
+
+    x_in, x_out = exchange(
+        xg.at[mine], through_x, lambda a: xg.at[(mine, partner)[a], a], ex_send.at[0], ex_recv.at[0]
+    )
     first_up, first_down = ag(4, mine, (0, 1), to_up), ag(8, mine, (0, 1), to_down)
-    for c in (over_x, first_up, first_down):
+    for c in (*x_in, first_up, first_down):
         c.start()
     second_up, second_down = ag(12, partner, (0, 1), to_up), ag(16, partner, (0, 1), to_down)
     fwd_up = [ag(20 + 2 * i, down * 2 + hh, (0,), to_up) for i, hh in enumerate((h, oh))]
     fwd_down = [ag(24 + 2 * i, up * 2 + hh, (1,), to_down) for i, hh in enumerate((h, oh))]
 
+    def target_of(j):
+        dz, dx, dc = j // 4, (j // 2) % 2, j % 2
+        return ((z + dz) % 4) * 4 + ((xl + dx) % 2) * 2 + (core + dc) % 2
+
     def a2a(j):
-        dz, dx, dc = j // 4, (j // 2) % 2, j % 2
-        target = ((z + dz) % 4) * 4 + ((xl + dx) % 2) * 2 + (core + dc) % 2
-        copy = remote(packed.at[j], got_ref.at[g], a2a_send.at[j], a2a_recv.at[j], {"group": target})
-        return target, copy
+        device = {"group": target_of(j)}
+        return remote(packed.at[j], got_ref.at[g], a2a_send.at[j], a2a_recv.at[j], device)
 
     def fill(j, target):
         row = 0
@@ -154,16 +172,35 @@
         for kv in range(2):
             packed[j, kv] = cache[row, kv]
 
-    def send_caches(along, across=()):
-        for dx, some in ((1, across), (0, along)):
-            for i in some:
-                j = (i // 2) * 4 + dx * 2 + i % 2
-                target, copy = a2a(j)
-                fill(j, target)
-                copy.start()
+    def send_caches(*rows):
+        for j in rows:
+            fill(j, target_of(j))
+            a2a(j).start()
+
+    z_next, z_last = ((z + 1) % 4) * 4 + xl * 2 + core, ((z + 3) % 4) * 4 + xl * 2 + core
+
+    def z_in(m, kv):
+        return remote(
+            packed.at[8 + m, kv], through_z.at[kv, m], zi_send.at[kv, m], zi_recv.at[kv, m],
+            {"group": (z_next, z_last)[kv]},
+        )
+
+    def z_out(m, kv):
+        onward, source = ((z_next // 4, z_last), (z_last // 4, z_next))[kv]
+        target = onward * 4 + ((xl + m // 2) % 2) * 2 + (core + m % 2) % 2
+        return remote(
+            through_z.at[kv, m], got_ref.at[source, kv], zo_send.at[kv, m], zo_recv.at[kv, m],
+            {"group": target},
+        )
+
+    halves_z = [(m, kv) for m in range(4) for kv in range(2)]
 
     loads[0].wait()
-    send_caches((1, 2, 6))
+    for m in range(4):
+        fill(8 + m, target_of(8 + m))
+        z_in(m, 0).start()
+        z_in(m, 1).start()
+    send_caches(1)
     fill(0, g)
     own_copy = pltpu.make_async_copy(packed.at[0], got_ref.at[g], a2a_send.at[0])
     own_copy.start()
@@ -326,19 +363,26 @@
         kt[:, rows] = k.astype(F32).T.astype(BF)
         vs[rows, :] = v[:, HD:].astype(BF)
 
+    for a in range(2):
+        x_in[a].wait_recv()
+        x_out[a].start()
     loads[1].wait()
     q0, new0 = dec_project(0, xin[...])
-    over_x.wait_recv()
+    for a in range(2):
+        x_out[a].wait_recv()
     second_up.start()
     second_down.start()
     first_up.wait_recv()
     fwd_up[0].start()
     first_down.wait_recv()
     fwd_down[0].start()
-    send_caches((3, 7), (0, 1))
+    send_caches(2, 3)
     w0, wf0 = dec_weights(q0, [new0])
     loads[3].wait()
     dec_out(0, w0, wf0, [new0])
+    for m, kv in halves_z:
+        z_in(m, kv).wait_recv()
+        z_out(m, kv).start()
     prepare(mine, 0)
     prepare(partner, 0)
     project(y)
@@ -353,7 +397,7 @@
     fwd_up[1].start()
     second_down.wait_recv()
     fwd_down[1].start()
-    send_caches((4,), (2, 3))
+    send_caches(6, 14, 4, 12)
     prepare(down * 2 + oh, 0)
     project(down)
     prepare(up * 2 + oh, 0)
@@ -367,7 +411,7 @@
     fwd_down[1].wait_recv()
     prepare(far * 2 + oh, 0)
     project(far)
-    send_caches((5,), (4, 5))
+    send_caches(7, 15)
 
     later_col = lax.broadcasted_iota(jnp.int32, (2 * SP, TOK), 1)
     later_row = lax.broadcasted_iota(jnp.int32, (2 * SP, TOK), 0)
@@ -405,7 +449,9 @@
         [rs(8 + 2 * i + a, terms.at[down * 2 + order[i], a], arrive.at[1, i, a], to_down) for a in range(2)]
         for i in range(2)
     ]
-    over = [rs(12 + a, cross.at[0, a], cross.at[1, a], to_x) for a in range(2)]
+    over_in, over = exchange(
+        cross.at[0], through_cross, lambda a: cross.at[1, a], ex_send.at[1], ex_recv.at[1]
+    )
 
     def relay_up(i):
         far_up[i].wait_recv()
@@ -439,7 +485,7 @@
     near_down[0][0].start()
     relay_up(0)
     relay_down(0)
-    send_caches((), (6, 7))
+    send_caches(5, 13)
     w1, wf1 = dec_weights(q1, [new0, new1])
     dec_out(1, w1, wf1, [new0, new1])
     attend(y)
@@ -449,7 +495,7 @@
     far_down[1].start()
     for a in range(2):
         cross[0, a] = summed(0, a).astype(BF)
-        over[a].start()
+        over_in[a].start()
 
     mine_rows = pl.ds(pl.multiple_of(g * RP, RP), RP)
     fin[mine_rows, 0:SL] = reduce_parts(1, xbuf[t])
@@ -468,6 +514,9 @@
     near_up[1][1].start()
     far_down[1].wait_send()
     near_down[1][0].start()
+    for a in range(2):
+        over_in[a].wait_recv()
+        over[a].start()
     relay_up(1)
     relay_down(1)
 
@@ -501,12 +550,16 @@
         dec_out_ref[:, p * SL : (p + 1) * SL] = obuf[p]
 
     def end_a2a(j, c):
-        a2a(j)[1].wait()
-        return c
-
-    lax.fori_loop(1, NG, end_a2a, 0)
+        a2a(j).wait()
+        return c
+
+    lax.fori_loop(1, 8, end_a2a, 0)
+    lax.fori_loop(12, NG, end_a2a, 0)
+    for m, kv in halves_z:
+        z_out(m, kv).wait()
     own_copy.wait()
-    ended = [over_x, first_up, first_down, second_up, second_down] + fwd_up + fwd_down + over
+    ended = [first_up, first_down, second_up, second_down] + fwd_up + fwd_down
+    ended += x_in + x_out + over_in + over + [z_in(m, kv) for m, kv in halves_z]
     ended += near_up[1] + near_down[1] + [near_up[0][1], near_down[0][0]]
     for c in ended:
         c.wait_send()
@@ -603,6 +656,9 @@
             pltpu.VMEM((2, 2, 2 * SH, QUART), BF),
             pltpu.VMEM((2, 2, 2, 2 * SH, QUART), BF),
             pltpu.VMEM((2, 2, 2 * SH, QUART), BF),
+            pltpu.VMEM((2, 2 * SH, QUART), BF),
+            pltpu.VMEM((2, 4, CTX, HD), BF),
+            pltpu.VMEM((2, 2 * SH, QUART), BF),
             pltpu.VMEM((SH, D), F32),
             pltpu.VMEM((2, NT, RP, SL), F32),
             pltpu.VMEM((2, NT, RP, SL), F32),
@@ -612,7 +668,7 @@
             pltpu.VMEM((RP, NG * RP), BF),
             pltpu.VMEM((NG * RP, MSG), BF),
             pltpu.VMEM((NT, RP, SL), BF),
-            dma((4,)), dma((NG,)), dma((NG,)), dma((28,)), dma((28,)), dma((42,)), dma((42,)),
+            dma((4,)), dma((NG,)), dma((NG,)), dma((2, 4)), dma((2, 4)), dma((2, 4)), dma((2, 4)), dma((2, 4)), dma((2, 4)), dma((28,)), dma((28,)), dma((42,)), dma((42,)),
             dma((2, NT)), dma((2, NT)), dma((NT,)), dma((NT,)), dma((NG,)), dma((NG,)),
             dma((NT,)), dma((NT,)),
         ],

time: 140 us -> 136 us (0.971)
  Pallas kernels: 139 us -> 135 us
    pallas_call x1, Pallas kernels: 132 us -> 128 us  [per_device(): pl.pallas_call(main_kernel, name='decode_and_score', out_shape=(jax.Shape...]
where the time goes in v4:
time: 136 us
  Pallas kernels  135 us (99%)
    pallas_call x1, Pallas kernels, per_device(): pl.pallas_call(main_kernel, name='decode_and_score', out_shape=(jax.Shape...  128 us
    pallas_call x1, Pallas kernels, per_device(): pl.pallas_call(place_kernel, name='place_rows', out_shape=(jax.ShapeDtype...  7.09 us

profile of v4, /device:TPU:0, one launch (start us, length us, event | category | flops | bytes accessed | tf_op | source)
XLA Modules:
  0.0 135.8 jit_solution(14810967971544677068)
XLA Ops:
  0.6 127.9 %decode_and_score.1 = (bf16[16,2,768,128]{3,2,1,0:T(8,128)(2,1)}, f32[16,512]{1,0:T(8,128)}, s32[16,128]{1,0:T(8,128)}, bf16[16,5120]{1,0:T(8,128)(2,1)}, bf16[56,5120]{1,0:T(8,128)(2,1)}) custom-call(s32[224]{0:T(256)} %dest_ref.1, s32[224]{0:T(256)} %slot_ref.1, s32[224]{0:T(256)} %len_ref.1, bf16[14,5120]{1,0:T(8,128)(2,1)} %dec_ref.1, ...), custom_call_target="tpu_custom_call" | custom-call | flops 8000000000 | bytes 30000000 | tf_op jit(solution)/shard_map/decode_and_score/pallas_call | solution.py:628
  128.5 7.1 %place_rows.1 = (bf16[14,5120]{1,0:T(8,128)(2,1)}, bf16[14,2,768,128]{3,2,1,0:T(8,128)(2,1)}, bf16[56,5120]{1,0:T(8,128)(2,1)}) custom-call(s32[16,128]{1,0:T(8,128)} %get-tuple-element.8.plan_ref, f32[16,512]{1,0:T(8,128)} %get-tuple-element.9.patch_ref, bf16[16,5120]{1,0:T(8,128)(2,1)} %get-tuple-element.10.dec_ref, ...), custom_call_target="tpu_custom_call" | custom-call | flops 1000000 | bytes 12000000 | tf_op jit(solution)/shard_map/place_rows/pallas_call | solution.py:684

commit v5 on v4

--- a/solution.py
+++ b/solution.py
@@ -29,6 +29,7 @@
 QUART = D // 4
 SL = D // NT
 MSG = SL + 4 * HD
+WAVE = 5
 GATHER_CUTS = ((0, 112),)
 SUM_CUTS = ((0, 112),)
 
@@ -65,10 +66,10 @@
 
 def main_kernel(
     dest_ref, slot_ref, len_ref,
-    dec_ref, score_ref, gain_ref, qgain_ref, kgain_ref, doc_ref,
-    cache_hbm, wq_hbm, wkv_hbm, wo_hbm,
+    gain_ref, qgain_ref, kgain_ref, doc_ref,
+    cache_hbm, wq_hbm, wkv_hbm, wo_hbm, score_hbm, dec_hbm,
     got_ref, patch_ref, plan_ref, dec_out_ref, score_out_ref,
-    cache, wkv, wqkv, wo, xin, docr_ref, docc_ref, packed, xg, xn, sc, qs, kt, vs, terms,
+    score_ref, dec_ref, cache, wkv, wqkv, wo, xin, docr_ref, docc_ref, packed, xg, xn, sc, qs, kt, vs, terms,
     relay, arrive, cross, through_x, through_z, through_cross, score_sum, part, gather_part, xbuf, nx, scores, pick, fin, obuf,
     load_sem, a2a_send, a2a_recv, ex_send, ex_recv, zi_send, zi_recv, zo_send, zo_recv, ag_send, ag_recv, rs_send, rs_recv,
     dp_send, dp_recv, dx_send, dx_recv, fin_send, fin_recv, o_send, o_recv,
@@ -90,29 +91,32 @@
             device_id=device, device_id_type=MESH,
         )
 
+    barrier = pltpu.get_barrier_semaphore()
+
+    def greet_tp(k, c):
+        pl.semaphore_signal(barrier, inc=1, device_id={"tp": (t + k) % NT}, device_id_type=MESH)
+        return c
+
+    def greet_group(k, c):
+        pl.semaphore_signal(barrier, inc=1, device_id={"group": (g + k) % NG}, device_id_type=MESH)
+        return c
+
+    lax.fori_loop(1, NT, greet_tp, 0)
+    lax.fori_loop(1, NG, greet_group, 0)
+    pl.semaphore_signal(barrier, inc=1, device_id=(g_x, partner), device_id_type=MESH)
+
     loads = [
         pltpu.make_async_copy(cache_hbm, cache, load_sem.at[0]),
         pltpu.make_async_copy(wq_hbm, wqkv.at[:, pl.ds(0, 512)], load_sem.at[1]),
         pltpu.make_async_copy(wkv_hbm, wkv, load_sem.at[2]),
         pltpu.make_async_copy(wo_hbm, wo, load_sem.at[3]),
+        pltpu.make_async_copy(score_hbm, score_ref, load_sem.at[4]),
+        pltpu.make_async_copy(dec_hbm, dec_ref, load_sem.at[5]),
     ]
-    for load in loads:
-        load.start()
-
-    barrier = pltpu.get_barrier_semaphore()
-
-    def greet_tp(k, c):
-        pl.semaphore_signal(barrier, inc=1, device_id={"tp": (t + k) % NT}, device_id_type=MESH)
-        return c
-
-    def greet_group(k, c):
-        pl.semaphore_signal(barrier, inc=1, device_id={"group": (g + k) % NG}, device_id_type=MESH)
-        return c
-
-    lax.fori_loop(1, NT, greet_tp, 0)
-    lax.fori_loop(1, NG, greet_group, 0)
-    pl.semaphore_signal(barrier, inc=1, device_id=(g_x, partner), device_id_type=MESH)
-
+    for i in (4, 0, 5, 2, 1, 3):
+        loads[i].start()
+
+    loads[4].wait()
     for a in range(2):
         lo = score_ref[:, a * HALF : a * HALF + QUART].astype(F32)
         hi = score_ref[:, a * HALF + QUART : (a + 1) * HALF].astype(F32)
@@ -205,6 +209,7 @@
     own_copy = pltpu.make_async_copy(packed.at[0], got_ref.at[g], a2a_send.at[0])
     own_copy.start()
 
+    loads[5].wait()
     xin[...] = jnp.zeros_like(xin)
     xin[0:R, :] = dec_ref[...].astype(F32)
     token = lax.broadcasted_iota(jnp.int32, (TOK, NT * SH), 1)
@@ -376,11 +381,14 @@
     fwd_up[0].start()
     first_down.wait_recv()
     fwd_down[0].start()
-    send_caches(2, 3)
+    send_caches(2)
+    for m, kv in halves_z[:4]:
+        z_in(m, kv).wait_recv()
+        z_out(m, kv).start()
     w0, wf0 = dec_weights(q0, [new0])
     loads[3].wait()
     dec_out(0, w0, wf0, [new0])
-    for m, kv in halves_z:
+    for m, kv in halves_z[4:]:
         z_in(m, kv).wait_recv()
         z_out(m, kv).start()
     prepare(mine, 0)
@@ -397,11 +405,12 @@
     fwd_up[1].start()
     second_down.wait_recv()
     fwd_down[1].start()
-    send_caches(6, 14, 4, 12)
+    send_caches(3, 6)
     prepare(down * 2 + oh, 0)
     project(down)
     prepare(up * 2 + oh, 0)
     project(up)
+    send_caches(14, 4)
     lax.fori_loop(1, NT, lambda k, c: (x_copy(k).wait_recv(), c)[1], 0)
     q1, new1 = dec_project(1, jnp.concatenate([xbuf[p] for p in range(NT)], axis=1))
     fwd_up[0].wait_recv()
@@ -411,7 +420,7 @@
     fwd_down[1].wait_recv()
     prepare(far * 2 + oh, 0)
     project(far)
-    send_caches(7, 15)
+    send_caches(7, 12)
 
     later_col = lax.broadcasted_iota(jnp.int32, (2 * SP, TOK), 1)
     later_row = lax.broadcasted_iota(jnp.int32, (2 * SP, TOK), 0)
@@ -478,6 +487,7 @@
     far_up[0].start()
     far_down[0].start()
     attend(up)
+    send_caches(15)
     attend(down)
     far_up[0].wait_send()
     near_up[0][1].start()
@@ -587,13 +597,18 @@
         pltpu.make_async_copy(got_hbm.at[plan_ref[s, 0]], rows.at[s], in_sem.at[s]).start()
         return c
 
-    lax.fori_loop(0, R, get, 0)
+    lax.fori_loop(0, WAVE, get, 0)
     dec_out_ref[...] = dec_ref[:R, :]
     score_in.wait()
     score_end.start()
 
     def put(s, c):
         pltpu.make_async_copy(got_hbm.at[0], rows.at[s], in_sem.at[s]).wait()
+
+        @pl.when(s + WAVE < R)
+        def _():
+            get(s + WAVE, 0)
+
         entry = patch_ref[pl.ds(s, 1), :]
         for step in range(2):
             pos = plan_ref[s, 1] + step
@@ -635,9 +650,11 @@
             jax.ShapeDtypeStruct((RP, D), BF),
             jax.ShapeDtypeStruct((SH, D), BF),
         ),
-        in_specs=[smem] * 3 + [vmem] * 6 + [hbm] * 4,
+        in_specs=[smem] * 3 + [vmem] * 4 + [hbm] * 6,
         out_specs=(hbm, vmem, vmem, vmem, vmem),
         scratch_shapes=[
+            pltpu.VMEM((SH, D), BF),
+            pltpu.VMEM((R, D), BF),
             pltpu.VMEM((R, 2, CTX, HD), BF),
             pltpu.VMEM((2 * D, HD), BF),
             pltpu.VMEM((D, 768), BF),
@@ -668,7 +685,7 @@
             pltpu.VMEM((RP, NG * RP), BF),
             pltpu.VMEM((NG * RP, MSG), BF),
             pltpu.VMEM((NT, RP, SL), BF),
-            dma((4,)), dma((NG,)), dma((NG,)), dma((2, 4)), dma((2, 4)), dma((2, 4)), dma((2, 4)), dma((2, 4)), dma((2, 4)), dma((28,)), dma((28,)), dma((42,)), dma((42,)),
+            dma((6,)), dma((NG,)), dma((NG,)), dma((2, 4)), dma((2, 4)), dma((2, 4)), dma((2, 4)), dma((2, 4)), dma((2, 4)), dma((28,)), dma((28,)), dma((42,)), dma((42,)),
             dma((2, NT)), dma((2, NT)), dma((NT,)), dma((NT,)), dma((NG,)), dma((NG,)),
             dma((NT,)), dma((NT,)),
         ],
@@ -677,9 +694,9 @@
         ),
         cost_estimate=pl.CostEstimate(flops=8 * 10**9, bytes_accessed=30 * 10**6, transcendentals=10**6),
     )(
-        dest_group, dest_slot, lengths, dec_rows, score_rows, norm_gain.reshape(1, D),
+        dest_group, dest_slot, lengths, norm_gain.reshape(1, D),
         query_gain.reshape(1, HD), key_gain.reshape(1, HD), doc_ids,
-        kv_cache, w_query, w_keyval.reshape(2 * D, HD), w_out,
+        kv_cache, w_query, w_keyval.reshape(2 * D, HD), w_out, score_rows, dec_rows,
     )
     return pl.pallas_call(
         place_kernel,

time: 136 us -> 136 us (level)
  no operation moved by 1% of the time
where the time goes in v5:
time: 136 us
  Pallas kernels  135 us (99%)
    pallas_call x1, Pallas kernels, per_device(): pl.pallas_call(main_kernel, name='decode_and_score', out_shape=(jax.Shape...  128 us
    pallas_call x1, Pallas kernels, per_device(): pl.pallas_call(place_kernel, name='place_rows', out_shape=(jax.ShapeDtype...  7.62 us

profile of v5, /device:TPU:0, one launch (start us, length us, event | category | flops | bytes accessed | tf_op | source)
XLA Modules:
  0.0 136.0 jit_solution(8055293531592906580)
XLA Ops:
  0.6 127.6 %decode_and_score.1 = (bf16[16,2,768,128]{3,2,1,0:T(8,128)(2,1)}, f32[16,512]{1,0:T(8,128)}, s32[16,128]{1,0:T(8,128)}, bf16[16,5120]{1,0:T(8,128)(2,1)}, bf16[56,5120]{1,0:T(8,128)(2,1)}) custom-call(s32[224]{0:T(256)} %dest_ref.1, s32[224]{0:T(256)} %slot_ref.1, s32[224]{0:T(256)} %len_ref.1, f32[1,5120]{1,0:T(1,128)} %bitcast.5, f32[1,128]{1,0:T(1,128)} %bitcast.6, ...), custom_call_target="tpu_custom_call" | custom-call | flops 8000000000 | bytes 30000000 | tf_op jit(solution)/shard_map/decode_and_score/pallas_call | solution.py:643
  128.3 7.6 %place_rows.1 = (bf16[14,5120]{1,0:T(8,128)(2,1)}, bf16[14,2,768,128]{3,2,1,0:T(8,128)(2,1)}, bf16[56,5120]{1,0:T(8,128)(2,1)}) custom-call(s32[16,128]{1,0:T(8,128)} %get-tuple-element.8.plan_ref, f32[16,512]{1,0:T(8,128)} %get-tuple-element.9.patch_ref, bf16[16,5120]{1,0:T(8,128)(2,1)} %get-tuple-element.10.dec_ref, ...), custom_call_target="tpu_custom_call" | custom-call | flops 1000000 | bytes 12000000 | tf_op jit(solution)/shard_map/place_rows/pallas_call | solution.py:701

commit v6 on v5

--- a/solution.py
+++ b/solution.py
@@ -29,7 +29,6 @@
 QUART = D // 4
 SL = D // NT
 MSG = SL + 4 * HD
-WAVE = 5
 GATHER_CUTS = ((0, 112),)
 SUM_CUTS = ((0, 112),)
 
@@ -69,7 +68,7 @@
     gain_ref, qgain_ref, kgain_ref, doc_ref,
     cache_hbm, wq_hbm, wkv_hbm, wo_hbm, score_hbm, dec_hbm,
     got_ref, patch_ref, plan_ref, dec_out_ref, score_out_ref,
-    score_ref, dec_ref, cache, wkv, wqkv, wo, xin, docr_ref, docc_ref, packed, xg, xn, sc, qs, kt, vs, terms,
+    score_ref, dec_ref, cache, wkv, wqkv, wo, xin, docr_ref, docc_ref, packed, xg, xn, sc, qs, ks, kt, vs, terms,
     relay, arrive, cross, through_x, through_z, through_cross, score_sum, part, gather_part, xbuf, nx, scores, pick, fin, obuf,
     load_sem, a2a_send, a2a_recv, ex_send, ex_recv, zi_send, zi_recv, zo_send, zo_recv, ag_send, ag_recv, rs_send, rs_recv,
     dp_send, dp_recv, dx_send, dx_recv, fin_send, fin_recv, o_send, o_recv,
@@ -250,16 +249,12 @@
     def stack4(v):
         return jnp.concatenate([v] * 4, axis=0)
 
-    def dec_project(step, x):
+    def dec_norm(x):
         wide = x.astype(F32)
-        scale = lax.rsqrt(jnp.mean(wide * wide, axis=-1, keepdims=True) + EPS)
         nx[...] = (wide * gain_ref[...]).astype(BF)
-
-        def chunk(k, acc):
-            cols = pl.ds(pl.multiple_of(k * 1024, 1024), 1024)
-            return acc + dot(nx[:, cols], wqkv[cols, :])
-
-        proj = lax.fori_loop(0, 5, chunk, jnp.zeros((RP, 768), F32)) * scale
+        return lax.rsqrt(jnp.mean(wide * wide, axis=-1, keepdims=True) + EPS)
+
+    def dec_heads(proj):
         q = jnp.concatenate([proj[:, i * HD : (i + 1) * HD] for i in range(4)], axis=0)
         q = head_norm(q, qgain_ref[...])
         return q, (head_norm(proj[:, 512:640], kgain_ref[...]), proj[:, 640:768].astype(BF))
@@ -288,7 +283,7 @@
         inv = 1.0 / total
         return (e * inv).astype(BF), [(f * inv).astype(BF).astype(F32) for f in ef]
 
-    def dec_out(step, w, wf, new):
+    def dec_attn(w, wf, new):
         def value_row(r, acc):
             return acc + jnp.where(row_of == r, dot(w, cache[r, 1]), 0.0)
 
@@ -296,13 +291,14 @@
         for f, (_, v) in zip(wf, new):
             o = o + f * stack4(v.astype(F32))
         o = o.astype(BF)
-        o = jnp.concatenate([o[i * RP : (i + 1) * RP] for i in range(4)], axis=1)
-
-        def out_slice(p, c):
-            part[step, p] = dot(o, wo[:, pl.ds(pl.multiple_of(p * SL, SL), SL)])
-            return c
-
-        lax.fori_loop(0, NT, out_slice, 0)
+        return jnp.concatenate([o[i * RP : (i + 1) * RP] for i in range(4)], axis=1)
+
+    def dec_out(step, o):
+        for p in range(NT):
+            part[step, p] = dot(o, wo[:, p * SL : (p + 1) * SL])
+        send_parts(step)
+
+    def send_parts(step):
         lax.fori_loop(1, NT, lambda k, c: (part_copy(step, k).start(), c)[1], 0)
 
     def part_copy(step, k):
@@ -353,26 +349,38 @@
         sc[rows, :] = jnp.broadcast_to(scale, (SP, HD))
         return c
 
-    def project(block):
-        rows = pl.ds(pl.multiple_of(block * 2 * SP, 2 * SP), 2 * SP)
-
-        def tile(j):
-            return dot(xn[rows, :], wqkv[:, j * 256 : (j + 1) * 256]) * sc[rows, 0:1]
-
-        for j in range(2):
-            v = tile(j)
-            for i in range(2):
-                qs[2 * j + i, rows, :] = head_norm(v[:, i * HD : (i + 1) * HD], qgain_ref[...])
-        v = tile(2)
-        k = head_norm(v[:, :HD], kgain_ref[...])
-        kt[:, rows] = k.astype(F32).T.astype(BF)
-        vs[rows, :] = v[:, HD:].astype(BF)
-
+    def project(shards, dec_scale=None):
+        spots = [pl.ds(pl.multiple_of(p * SP, SP), SP) for p in shards]
+        lhs = [xn[rows, :] for rows in spots]
+        scale = [sc[rows, 0:1] for rows in spots]
+        if dec_scale is not None:
+            lhs.append(nx[...])
+            scale.append(dec_scale)
+        lhs = jnp.concatenate(lhs, axis=0)
+        scale = jnp.concatenate(scale, axis=0)
+        extra = []
+        for j in range(3):
+            v = dot(lhs, wqkv[:, j * 256 : (j + 1) * 256]) * scale
+            extra.append(v[len(shards) * SP :])
+            for n, rows in enumerate(spots):
+                mine_v = v[n * SP : (n + 1) * SP]
+                if j < 2:
+                    for i in range(2):
+                        head = mine_v[:, i * HD : (i + 1) * HD]
+                        qs[2 * j + i, rows, :] = head_norm(head, qgain_ref[...])
+                else:
+                    ks[rows, :] = head_norm(mine_v[:, :HD], kgain_ref[...]).astype(F32)
+                    vs[rows, :] = mine_v[:, HD:].astype(BF)
+        if dec_scale is not None:
+            return dec_heads(jnp.concatenate(extra, axis=1))
+
+    prepare(mine, 0)
+    scale0 = dec_norm(xin[...])
     for a in range(2):
         x_in[a].wait_recv()
         x_out[a].start()
     loads[1].wait()
-    q0, new0 = dec_project(0, xin[...])
+    q0, new0 = project((mine,), scale0)
     for a in range(2):
         x_out[a].wait_recv()
     second_up.start()
@@ -387,15 +395,14 @@
         z_out(m, kv).start()
     w0, wf0 = dec_weights(q0, [new0])
     loads[3].wait()
-    dec_out(0, w0, wf0, [new0])
+    dec_out(0, dec_attn(w0, wf0, [new0]))
     for m, kv in halves_z[4:]:
         z_in(m, kv).wait_recv()
         z_out(m, kv).start()
-    prepare(mine, 0)
     prepare(partner, 0)
-    project(y)
     prepare(down * 2 + h, 0)
     prepare(up * 2 + h, 0)
+    project((partner, down * 2 + h, up * 2 + h))
 
     base0 = xin[:, pl.ds(pl.multiple_of(t * SL, SL), SL)]
     xbuf[t] = reduce_parts(0, base0)
@@ -407,25 +414,25 @@
     fwd_down[1].start()
     send_caches(3, 6)
     prepare(down * 2 + oh, 0)
-    project(down)
     prepare(up * 2 + oh, 0)
-    project(up)
+    lax.fori_loop(1, NT, lambda k, c: (x_copy(k).wait_recv(), c)[1], 0)
+    scale1 = dec_norm(jnp.concatenate([xbuf[p] for p in range(NT)], axis=1))
+    q1, new1 = project((down * 2 + oh, up * 2 + oh), scale1)
     send_caches(14, 4)
-    lax.fori_loop(1, NT, lambda k, c: (x_copy(k).wait_recv(), c)[1], 0)
-    q1, new1 = dec_project(1, jnp.concatenate([xbuf[p] for p in range(NT)], axis=1))
     fwd_up[0].wait_recv()
     fwd_down[0].wait_recv()
     prepare(far * 2 + h, 0)
     fwd_up[1].wait_recv()
     fwd_down[1].wait_recv()
     prepare(far * 2 + oh, 0)
-    project(far)
+    project((far * 2 + h, far * 2 + oh))
+    kt[...] = ks[...].T.astype(BF)
     send_caches(7, 12)
 
     later_col = lax.broadcasted_iota(jnp.int32, (2 * SP, TOK), 1)
     later_row = lax.broadcasted_iota(jnp.int32, (2 * SP, TOK), 0)
 
-    def attend(block):
+    def heads_of(block):
         rows = pl.ds(pl.multiple_of(block * 2 * SP, 2 * SP), 2 * SP)
         live = (docc_ref[rows, 0:1] == docr_ref[0:1, :]) & (later_col <= later_row + block * (2 * SP))
         heads = []
@@ -434,14 +441,27 @@
             e = jnp.exp(s - jnp.max(s, axis=-1, keepdims=True))
             inv = 1.0 / jnp.sum(e, axis=-1, keepdims=True)
             heads.append(dot((e * inv).astype(BF), vs[...]).astype(BF))
-        attn = jnp.concatenate(heads, axis=1)
+        return jnp.concatenate(heads, axis=1)
+
+    def attend(blocks, dec=None):
+        attn = [heads_of(block) for block in blocks]
+        if dec is not None:
+            attn.append(dec)
+        attn = jnp.concatenate(attn, axis=0)
         for a in range(2):
             lo, hi = [
                 dot(attn, wo[:, a * HALF + i * QUART : a * HALF + (i + 1) * QUART]) for i in range(2)
             ]
-            for i in range(2):
-                pair = [v[i * SP : i * SP + SH] for v in (lo, hi)]
-                terms[block * 2 + i, a] = jnp.concatenate(pair, axis=0).astype(BF)
+            for n, block in enumerate(blocks):
+                for i in range(2):
+                    start = (2 * n + i) * SP
+                    pair = [v[start : start + SH] for v in (lo, hi)]
+                    terms[block * 2 + i, a] = jnp.concatenate(pair, axis=0).astype(BF)
+            if dec is not None:
+                start = len(blocks) * 2 * SP
+                for i, v in enumerate((lo, hi)):
+                    for k in range(2):
+                        part[1, 4 * a + 2 * i + k] = v[start:, k * SL : (k + 1) * SL]
 
     order = (oh, h)
 
@@ -483,12 +503,11 @@
             + arrive[1, i, a].astype(F32)
         )
 
-    attend(far)
+    attend((far,))
     far_up[0].start()
     far_down[0].start()
-    attend(up)
+    attend((up, down))
     send_caches(15)
-    attend(down)
     far_up[0].wait_send()
     near_up[0][1].start()
     far_down[0].wait_send()
@@ -497,8 +516,8 @@
     relay_down(0)
     send_caches(5, 13)
     w1, wf1 = dec_weights(q1, [new0, new1])
-    dec_out(1, w1, wf1, [new0, new1])
-    attend(y)
+    attend((y,), dec_attn(w1, wf1, [new0, new1]))
+    send_parts(1)
     near_up[0][0].wait_send()
     far_up[1].start()
     near_down[0][1].wait_send()
@@ -597,18 +616,13 @@
         pltpu.make_async_copy(got_hbm.at[plan_ref[s, 0]], rows.at[s], in_sem.at[s]).start()
         return c
 
-    lax.fori_loop(0, WAVE, get, 0)
+    lax.fori_loop(0, R, get, 0)
     dec_out_ref[...] = dec_ref[:R, :]
     score_in.wait()
     score_end.start()
 
     def put(s, c):
         pltpu.make_async_copy(got_hbm.at[0], rows.at[s], in_sem.at[s]).wait()
-
-        @pl.when(s + WAVE < R)
-        def _():
-            get(s + WAVE, 0)
-
         entry = patch_ref[pl.ds(s, 1), :]
         for step in range(2):
             pos = plan_ref[s, 1] + step
@@ -667,6 +681,7 @@
             pltpu.VMEM((TOK, D), BF),
             pltpu.VMEM((TOK, HD), F32),
             pltpu.VMEM((4, TOK, HD), BF),
+            pltpu.VMEM((TOK, HD), F32),
             pltpu.VMEM((HD, TOK), BF),
             pltpu.VMEM((TOK, HD), BF),
             pltpu.VMEM((NT, 2, 2 * SH, QUART), BF),

time: 136 us -> 136 us (level)
  no operation moved by 1% of the time
where the time goes in v6:
time: 136 us
  Pallas kernels  135 us (99%)
    pallas_call x1, Pallas kernels, per_device(): pl.pallas_call(main_kernel, name='decode_and_score', out_shape=(jax.Shape...  128 us
    pallas_call x1, Pallas kernels, per_device(): pl.pallas_call(place_kernel, name='place_rows', out_shape=(jax.ShapeDtype...  7.09 us

profile of v6, /device:TPU:0, one launch (start us, length us, event | category | flops | bytes accessed | tf_op | source)
XLA Modules:
  0.0 135.6 jit_solution(9394095836016116849)
XLA Ops:
  0.6 127.7 %decode_and_score.1 = (bf16[16,2,768,128]{3,2,1,0:T(8,128)(2,1)}, f32[16,512]{1,0:T(8,128)}, s32[16,128]{1,0:T(8,128)}, bf16[16,5120]{1,0:T(8,128)(2,1)}, bf16[56,5120]{1,0:T(8,128)(2,1)}) custom-call(s32[224]{0:T(256)} %dest_ref.1, s32[224]{0:T(256)} %slot_ref.1, s32[224]{0:T(256)} %len_ref.1, f32[1,5120]{1,0:T(1,128)} %bitcast.5, f32[1,128]{1,0:T(1,128)} %bitcast.6, ...), custom_call_target="tpu_custom_call" | custom-call | flops 8000000000 | bytes 30000000 | tf_op jit(solution)/shard_map/decode_and_score/pallas_call | solution.py:657
  128.3 7.1 %place_rows.1 = (bf16[14,5120]{1,0:T(8,128)(2,1)}, bf16[14,2,768,128]{3,2,1,0:T(8,128)(2,1)}, bf16[56,5120]{1,0:T(8,128)(2,1)}) custom-call(s32[16,128]{1,0:T(8,128)} %get-tuple-element.8.plan_ref, f32[16,512]{1,0:T(8,128)} %get-tuple-element.9.patch_ref, bf16[16,5120]{1,0:T(8,128)(2,1)} %get-tuple-element.10.dec_ref, ...), custom_call_target="tpu_custom_call" | custom-call | flops 1000000 | bytes 12000000 | tf_op jit(solution)/shard_map/place_rows/pallas_call | solution.py:716

commit v7 on v6

--- a/solution.py
+++ b/solution.py
@@ -69,7 +69,7 @@
     cache_hbm, wq_hbm, wkv_hbm, wo_hbm, score_hbm, dec_hbm,
     got_ref, patch_ref, plan_ref, dec_out_ref, score_out_ref,
     score_ref, dec_ref, cache, wkv, wqkv, wo, xin, docr_ref, docc_ref, packed, xg, xn, sc, qs, ks, kt, vs, terms,
-    relay, arrive, cross, through_x, through_z, through_cross, score_sum, part, gather_part, xbuf, nx, scores, pick, fin, obuf,
+    relay, arrive, cross, through_x, through_z, through_cross, score_sum, part, gather_part, xbuf, nx, scores, pick, drop, fin, arrived, obuf,
     load_sem, a2a_send, a2a_recv, ex_send, ex_recv, zi_send, zi_recv, zo_send, zo_recv, ag_send, ag_recv, rs_send, rs_recv,
     dp_send, dp_recv, dx_send, dx_recv, fin_send, fin_recv, o_send, o_recv,
 ):
@@ -219,6 +219,8 @@
     docr_ref[...] = dot_t(ids[:16], spread)
     docc_ref[...] = dot_t(spread, ids)
 
+    fin[...] = jnp.zeros_like(fin)
+
     lane = lax.broadcasted_iota(jnp.int32, (RP, NG * RP), 1)
     slot_row = lax.broadcasted_iota(jnp.int32, (RP, NG * RP), 0)
 
@@ -233,10 +235,15 @@
 
     none = jnp.full((RP, NG * RP), -1, jnp.int32)
     want, span = lax.fori_loop(0, NG, wanted, (none, jnp.zeros_like(none)))
-    pick[...] = (want == slot_row).astype(F32).astype(BF)
     source = jnp.sum(jnp.where(want == slot_row, lane >> 4, 0), axis=-1, keepdims=True)
     length = jnp.sum(jnp.where(want == slot_row, span, 0), axis=-1, keepdims=True)
     plan_lane = lax.broadcasted_iota(jnp.int32, (RP, HD), 1)
+    pick[...] = (source == plan_lane).astype(F32).astype(BF)
+    row_dest = jnp.full((RP, HD), -1, jnp.int32)
+    for r in range(R):
+        row_dest = jnp.where(plan_lane == r, dest_ref[g * R + r], row_dest)
+    outward = row_dest == lax.broadcasted_iota(jnp.int32, (RP, HD), 0)
+    drop[...] = outward.astype(F32).astype(BF)
     plan_ref[...] = jnp.where(plan_lane == 0, source, length)
 
     row_of = lax.broadcasted_iota(jnp.int32, (4 * RP, HD), 0) & (RP - 1)
@@ -526,16 +533,17 @@
         cross[0, a] = summed(0, a).astype(BF)
         over_in[a].start()
 
-    mine_rows = pl.ds(pl.multiple_of(g * RP, RP), RP)
-    fin[mine_rows, 0:SL] = reduce_parts(1, xbuf[t])
-    for i, (k, v) in enumerate([new0, new1]):
-        start = SL + 2 * i * HD
-        fin[mine_rows, start : start + HD] = k
-        fin[mine_rows, start + HD : start + 2 * HD] = v
+    columns = [reduce_parts(1, xbuf[t])]
+    for k, v in (new0, new1):
+        columns += [k, v]
+    leaving = dot(drop[:, :RP], jnp.concatenate(columns, axis=1))
+    for i in range(MSG // HD):
+        fin[:, i, :] = leaving[:, i * HD : (i + 1) * HD]
+    arrived[g] = fin[g]
 
     def fin_copy(k):
-        where = fin.at[mine_rows]
-        return remote(where, where, fin_send.at[k], fin_recv.at[k], {"group": (g + k) % NG})
+        target = (g + k) % NG
+        return remote(fin.at[target], arrived.at[g], fin_send.at[k], fin_recv.at[k], {"group": target})
 
     lax.fori_loop(1, NG, lambda k, c: (fin_copy(k).start(), c)[1], 0)
 
@@ -557,9 +565,9 @@
             score_sum[:, cols] = score_ref[:, cols].astype(F32) + add
 
     lax.fori_loop(1, NG, lambda k, c: (fin_copy(k).wait_recv(), c)[1], 0)
-    placed = dot(pick[...], fin[...])
-    obuf[t] = placed[:, :SL].astype(BF)
-    patch_ref[...] = placed[:, SL:]
+    placed = [dot(pick[:, :NG], arrived[:, i, :].astype(BF)) for i in range(MSG // HD)]
+    obuf[t] = jnp.concatenate(placed[: SL // HD], axis=1).astype(BF)
+    patch_ref[...] = jnp.concatenate(placed[SL // HD :], axis=1)
 
     def o_copy(k):
         return remote(obuf.at[t], obuf.at[t], o_send.at[k], o_recv.at[k], {"tp": (t + k) % NT})
@@ -697,8 +705,10 @@
             pltpu.VMEM((NT, RP, SL), BF),
             pltpu.VMEM((RP, D), BF),
             pltpu.VMEM((4 * RP, CTX), F32),
-            pltpu.VMEM((RP, NG * RP), BF),
-            pltpu.VMEM((NG * RP, MSG), BF),
+            pltpu.VMEM((RP, HD), BF),
+            pltpu.VMEM((RP, HD), BF),
+            pltpu.VMEM((NG, RP, HD), F32),
+            pltpu.VMEM((NG, RP, HD), F32),
             pltpu.VMEM((NT, RP, SL), BF),
             dma((6,)), dma((NG,)), dma((NG,)), dma((2, 4)), dma((2, 4)), dma((2, 4)), dma((2, 4)), dma((2, 4)), dma((2, 4)), dma((28,)), dma((28,)), dma((42,)), dma((42,)),
             dma((2, NT)), dma((2, NT)), dma((NT,)), dma((NT,)), dma((NG,)), dma((NG,)),

time: 136 us -> 135 us (level)
  no operation moved by 1% of the time
where the time goes in v7:
time: 135 us
  Pallas kernels  134 us (99%)
    pallas_call x1, Pallas kernels, per_device(): pl.pallas_call(main_kernel, name='decode_and_score', out_shape=(jax.Shape...  127 us
    pallas_call x1, Pallas kernels, per_device(): pl.pallas_call(place_kernel, name='place_rows', out_shape=(jax.ShapeDtype...  7.09 us

profile of v7, /device:TPU:0, one launch (start us, length us, event | category | flops | bytes accessed | tf_op | source)
XLA Modules:
  0.0 134.6 jit_solution(14329249006256192211)
XLA Ops:
  0.6 126.7 %decode_and_score.1 = (bf16[16,2,768,128]{3,2,1,0:T(8,128)(2,1)}, f32[16,512]{1,0:T(8,128)}, s32[16,128]{1,0:T(8,128)}, bf16[16,5120]{1,0:T(8,128)(2,1)}, bf16[56,5120]{1,0:T(8,128)(2,1)}) custom-call(s32[224]{0:T(256)} %dest_ref.1, s32[224]{0:T(256)} %slot_ref.1, s32[224]{0:T(256)} %len_ref.1, f32[1,5120]{1,0:T(1,128)} %bitcast.5, f32[1,128]{1,0:T(1,128)} %bitcast.6, ...), custom_call_target="tpu_custom_call" | custom-call | flops 8000000000 | bytes 30000000 | tf_op jit(solution)/shard_map/decode_and_score/pallas_call | solution.py:665
  127.4 7.1 %place_rows.1 = (bf16[14,5120]{1,0:T(8,128)(2,1)}, bf16[14,2,768,128]{3,2,1,0:T(8,128)(2,1)}, bf16[56,5120]{1,0:T(8,128)(2,1)}) custom-call(s32[16,128]{1,0:T(8,128)} %get-tuple-element.8.plan_ref, f32[16,512]{1,0:T(8,128)} %get-tuple-element.9.patch_ref, bf16[16,5120]{1,0:T(8,128)(2,1)} %get-tuple-element.10.dec_ref, ...), custom_call_target="tpu_custom_call" | custom-call | flops 1000000 | bytes 12000000 | tf_op jit(solution)/shard_map/place_rows/pallas_call | solution.py:726

commit v8 on v7

--- a/solution.py
+++ b/solution.py
@@ -396,7 +396,7 @@
     fwd_up[0].start()
     first_down.wait_recv()
     fwd_down[0].start()
-    send_caches(2)
+    send_caches(2, 4)
     for m, kv in halves_z[:4]:
         z_in(m, kv).wait_recv()
         z_out(m, kv).start()
@@ -419,13 +419,13 @@
     fwd_up[1].start()
     second_down.wait_recv()
     fwd_down[1].start()
-    send_caches(3, 6)
+    send_caches(3, 6, 12)
     prepare(down * 2 + oh, 0)
     prepare(up * 2 + oh, 0)
     lax.fori_loop(1, NT, lambda k, c: (x_copy(k).wait_recv(), c)[1], 0)
     scale1 = dec_norm(jnp.concatenate([xbuf[p] for p in range(NT)], axis=1))
     q1, new1 = project((down * 2 + oh, up * 2 + oh), scale1)
-    send_caches(14, 4)
+    send_caches(14, 5)
     fwd_up[0].wait_recv()
     fwd_down[0].wait_recv()
     prepare(far * 2 + h, 0)
@@ -434,7 +434,7 @@
     prepare(far * 2 + oh, 0)
     project((far * 2 + h, far * 2 + oh))
     kt[...] = ks[...].T.astype(BF)
-    send_caches(7, 12)
+    send_caches(7, 13)
 
     later_col = lax.broadcasted_iota(jnp.int32, (2 * SP, TOK), 1)
     later_row = lax.broadcasted_iota(jnp.int32, (2 * SP, TOK), 0)
@@ -521,7 +521,6 @@
     near_down[0][0].start()
     relay_up(0)
     relay_down(0)
-    send_caches(5, 13)
     w1, wf1 = dec_weights(q1, [new0, new1])
     attend((y,), dec_attn(w1, wf1, [new0, new1]))
     send_parts(1)

time: 135 us -> 135 us (level)
  no operation moved by 1% of the time
where the time goes in v8:
time: 135 us
  Pallas kernels  134 us (99%)
    pallas_call x1, Pallas kernels, per_device(): pl.pallas_call(main_kernel, name='decode_and_score', out_shape=(jax.Shape...  127 us
    pallas_call x1, Pallas kernels, per_device(): pl.pallas_call(place_kernel, name='place_rows', out_shape=(jax.ShapeDtype...  7.09 us

profile of v8, /device:TPU:0, one launch (start us, length us, event | category | flops | bytes accessed | tf_op | source)
XLA Modules:
  0.0 134.5 jit_solution(10628049445511609304)
XLA Ops:
  0.6 126.6 %decode_and_score.1 = (bf16[16,2,768,128]{3,2,1,0:T(8,128)(2,1)}, f32[16,512]{1,0:T(8,128)}, s32[16,128]{1,0:T(8,128)}, bf16[16,5120]{1,0:T(8,128)(2,1)}, bf16[56,5120]{1,0:T(8,128)(2,1)}) custom-call(s32[224]{0:T(256)} %dest_ref.1, s32[224]{0:T(256)} %slot_ref.1, s32[224]{0:T(256)} %len_ref.1, f32[1,5120]{1,0:T(1,128)} %bitcast.5, f32[1,128]{1,0:T(1,128)} %bitcast.6, ...), custom_call_target="tpu_custom_call" | custom-call | flops 8000000000 | bytes 30000000 | tf_op jit(solution)/shard_map/decode_and_score/pallas_call | solution.py:664
  127.3 7.1 %place_rows.1 = (bf16[14,5120]{1,0:T(8,128)(2,1)}, bf16[14,2,768,128]{3,2,1,0:T(8,128)(2,1)}, bf16[56,5120]{1,0:T(8,128)(2,1)}) custom-call(s32[16,128]{1,0:T(8,128)} %get-tuple-element.8.plan_ref, f32[16,512]{1,0:T(8,128)} %get-tuple-element.9.patch_ref, bf16[16,5120]{1,0:T(8,128)(2,1)} %get-tuple-element.10.dec_ref, ...), custom_call_target="tpu_custom_call" | custom-call | flops 1000000 | bytes 12000000 | tf_op jit(solution)/shard_map/place_rows/pallas_call | solution.py:725
